TPU v7x, 512 devices: a whole 4x4x16 slice. The times are simulated.
512 devices in a mesh: pipe: 32 (over z, x_lo), section: 8 (over x_hi, y), tensor: 2 (over core).
Axes of the slice: x: 4 (x_hi: 2, x_lo: 2; x = x_hi * 2 + x_lo), y: 4, z: 16, core: 2. Of those that a mesh axis runs over, the one named last changes fastest.
Arguments:
- stashed: bfloat16 [32, 8, 4, 48, 6144], P('pipe', 'section', None, None, 'tensor'), may hold values from -6 to 6
- cotangent: bfloat16 [32, 8, 4, 48, 6144], P('pipe', 'section', None, None, 'tensor'), may hold values from -3 to 3
- down_weight: bfloat16 [12, 2, 3072, 128], P(None, 'tensor', 'pipe'), may hold values from -0.078125 to 0.078125
- up_weight: bfloat16 [12, 2, 3072, 128], P(None, 'tensor', 'pipe'), may hold values from -0.5 to 0.5
- layer_split: int32 [16, 8], replicated, may hold values from 1 to 2, as said below
- template_of: int32 [32], replicated, may hold values from 0 to 15
- mb_count: int32 [32], replicated, may hold values from 1 to 4, 80 in all
Outputs:
- grad_down: float32 [12, 2, 3072, 128], P(None, 'tensor', ('pipe', 'section'))
- grad_up: float32 [12, 2, 3072, 128], P(None, 'tensor', ('pipe', 'section'))
Inputs may be any that keep to these rules, and one draw needn't show every extreme that they name: `layer_split`: each row gives the consecutive layers held by the 8 sections of a template, in section order, and sums to 12. The first mb_count[p] microbatch slots of relay p are live.
All inputs are finite; a program needn't handle non-finite values.
Results may differ from a plain program's by a relative error of at most 0.006.
Values may be sent and summed in bfloat16 or wider, within the bound.
A program may use at most 64 MiB of HBM per device.

v0:
```python
import jax
import jax.numpy as jnp
from jax import lax
from jax.sharding import PartitionSpec as P

SLOTS = 2


gelu_scale = 0.7978845608028654
gelu_cubic = 0.044715


def gelu_value(values):
    inner = jnp.tanh(gelu_scale * (values + gelu_cubic * values * values * values))
    return 0.5 * values * (1.0 + inner)


def gelu_slope(values):
    inner = jnp.tanh(gelu_scale * (values + gelu_cubic * values * values * values))
    return 0.5 * (1.0 + inner) + 0.5 * values * (1.0 - inner * inner) * gelu_scale * (
        1.0 + 3.0 * gelu_cubic * values * values
    )


def contract_rows(left, right):
    return lax.dot_general(
        left, right, (((0,), (0,)), ((), ())), preferred_element_type=jnp.float32
    )


def contract_last(left, right):
    return lax.dot_general(
        left, right, (((1,), (1,)), ((), ())), preferred_element_type=jnp.float32
    )


def pick_column(table, index):
    marked = jnp.arange(table.shape[1])[None, :] == index
    return jnp.sum(jnp.where(marked, table, 0), axis=1)


def pick_entry(vector, index):
    marked = jnp.arange(vector.shape[0]) == index
    return jnp.sum(jnp.where(marked, vector, 0))


def hidden_pre(section_rows, weight):
    return lax.psum(jnp.dot(section_rows, weight, preferred_element_type=jnp.float32), "tensor")


def hidden_back(incoming, weight):
    return lax.psum(jnp.dot(incoming, weight, preferred_element_type=jnp.float32), "tensor")


def local(stashed, cotangent, down_weight, up_weight, layer_split, template_of, mb_count):
    pipe_count = lax.axis_size("pipe")
    pipe_at = lax.axis_index("pipe")
    section_at = lax.axis_index("section")
    layer_count = down_weight.shape[0]
    row_block = down_weight.shape[2]
    bottleneck = down_weight.shape[3]
    micro_rows = stashed.shape[3]
    row_count = stashed.shape[2] * micro_rows
    half_width = stashed.shape[4]
    template_count = layer_split.shape[0]
    chooser = template_of[:, None] == jnp.arange(template_count)[None, :]
    chosen = jnp.sum(jnp.where(chooser[:, :, None], layer_split[None, :, :], 0), axis=1)
    firsts = jnp.cumsum(chosen, axis=1) - chosen
    first_column = pick_column(firsts, section_at)
    count_column = pick_column(chosen, section_at)
    holds_two = pick_entry(count_column, pipe_at) > 1
    live_count = pick_entry(mb_count, pipe_at)
    slot_ids = jnp.arange(SLOTS)
    wanted = jnp.minimum(first_column[:, None] + slot_ids[None, :], layer_count - 1)
    send_down = jnp.take(down_weight[:, 0], wanted, axis=0)
    send_up = jnp.take(up_weight[:, 0], wanted, axis=0)
    section_rows = stashed.reshape(row_count, half_width)
    live_rows = jnp.arange(row_count) // micro_rows < live_count
    incoming = jnp.where(
        live_rows[:, None], cotangent.reshape(row_count, half_width), jnp.zeros((), jnp.bfloat16)
    )
    got_down, got_up = (
        lax.all_to_all(send_down, "pipe", split_axis=0, concat_axis=2, tiled=True),
        lax.all_to_all(send_up, "pipe", split_axis=0, concat_axis=2, tiled=True),
    )
    down_zero, up_zero = (got_down[0, 0], got_up[0, 0])
    down_one, up_one = (got_down[0, 1], got_up[0, 1])
    pre_zero = hidden_pre(section_rows, down_zero)
    act_zero = gelu_value(pre_zero).astype(jnp.bfloat16)
    input_one = (section_rows.astype(jnp.float32) + contract_last(act_zero, up_zero)).astype(
        jnp.bfloat16
    )
    pre_one = hidden_pre(input_one, down_one)
    act_one = gelu_value(pre_one).astype(jnp.bfloat16)
    back_one = hidden_back(incoming, up_one)
    slope_one = (back_one * gelu_slope(pre_one)).astype(jnp.bfloat16)
    term_down_one = contract_rows(input_one, slope_one).astype(jnp.bfloat16)
    term_up_one = contract_rows(incoming, act_one).astype(jnp.bfloat16)
    passed = (incoming.astype(jnp.float32) + contract_last(slope_one, down_one)).astype(
        jnp.bfloat16
    )
    cot_zero = jnp.where(holds_two, passed, incoming)
    back_zero = hidden_back(cot_zero, up_zero)
    slope_zero = (back_zero * gelu_slope(pre_zero)).astype(jnp.bfloat16)
    term_down_zero = contract_rows(section_rows, slope_zero).astype(jnp.bfloat16)
    term_up_zero = contract_rows(cot_zero, act_zero).astype(jnp.bfloat16)
    stacked_down = jnp.stack([term_down_zero, term_down_one]).reshape(
        SLOTS, pipe_count, row_block, bottleneck
    )
    stacked_up = jnp.stack([term_up_zero, term_up_one]).reshape(
        SLOTS, pipe_count, row_block, bottleneck
    )
    recv_down, recv_up = (
        lax.all_to_all(stacked_down, "pipe", split_axis=1, concat_axis=0, tiled=True),
        lax.all_to_all(stacked_up, "pipe", split_axis=1, concat_axis=0, tiled=True),
    )
    recv_down = recv_down.reshape(pipe_count, SLOTS, row_block, bottleneck)
    recv_up = recv_up.reshape(pipe_count, SLOTS, row_block, bottleneck)
    source_layer = first_column[:, None] + slot_ids[None, :]
    source_valid = slot_ids[None, :] < count_column[:, None]
    matches = source_layer[None, :, :] == jnp.arange(layer_count)[:, None, None]
    gather_sel = jnp.logical_and(matches, source_valid[None, :, :]).astype(jnp.bfloat16)
    table_down = jnp.einsum(
        "lpk,pkxr->lxr", gather_sel, recv_down, preferred_element_type=jnp.float32
    )
    table_up = jnp.einsum("lpk,pkxr->lxr", gather_sel, recv_up, preferred_element_type=jnp.float32)
    summed_down, summed_up = (
        lax.psum_scatter(table_down, "section", scatter_dimension=1, tiled=True),
        lax.psum_scatter(table_up, "section", scatter_dimension=1, tiled=True),
    )
    total_count = jnp.sum(mb_count).astype(jnp.float32)
    return ((summed_down / total_count)[:, None], (summed_up / total_count)[:, None])


def solution(mesh):
    placed = (
        P("pipe", "section", None, None, "tensor"),
        P("pipe", "section", None, None, "tensor"),
        P(None, "tensor", "pipe", None),
        P(None, "tensor", "pipe", None),
        P(),
        P(),
        P(),
    )
    return jax.shard_map(
        local,
        mesh=mesh,
        in_specs=placed,
        out_specs=(
            P(None, "tensor", ("pipe", "section"), None),
            P(None, "tensor", ("pipe", "section"), None),
        ),
        check_vma=False,
    )
```

profile of v0, /device:TPU:8, one launch (start us, length us, event | category | flops | bytes accessed | tf_op | source)
XLA Modules:
  0.0 567.1 jit_solution(16837896050706157939)
XLA Ops:
  7.2 0.8 copy.63
  8.0 0.7 iota_compare_fusion.1
  9.2 0.9 gather_fusion.1
  10.2 1.9 gather_fusion
  12.1 2.9 broadcast_select_fusion
  15.0 94.1 %all_to_all.66 = bf16[32,2,96,128]{3,2,1,0:T(8,128)(2,1)S(1)} all-to-all(bf16[32,2,96,128]{3,2,1,0:T(8,128)(2,1)S(1)} %get-tuple-element.22), channel_id=1, replica_groups=mesh['pipe'=32,'section'=8,'tensor'=2] {'pipe'}, dimensions={0} | all-to-all | bytes 3145728 | tf_op jit(solution)/shard_map/all_to_all | solution.py:84
  109.0 4.1 all-to-all-start.1
  113.2 0.6 fusion.65
  113.8 0.7 fusion.51
  114.5 0.7 fusion.53
  115.2 2.5 broadcast_select_fusion.2
  117.6 1.3 copy.66
  118.9 69.0 %all-to-all-done.1 = bf16[32,2,96,128]{3,2,1,0:T(8,128)(2,1)S(1)} async-done(((bf16[32,2,96,128]{3,2,1,0:T(8,128)(2,1)}), bf16[32,2,96,128]{3,2,1,0:T(8,128)(2,1)S(1)}, u32[]{:S(2)}, u32[]{:S(2)}) %all-to-all-start.1) | async-done | bytes 1572896 | tf_op jit(solution)/shard_map/all_to_all | solution.py:83
  188.0 1.1 copy-done.9
  189.1 0.6 copy-done.3
  189.7 1.1 convolution_bitcast_fusion
  190.9 2.4 fusion.16
  193.3 30.2 %all-reduce.5.cloned.1.call-done = f32[192,128]{1,0:T(8,128)} async-done(((f32[192,128]{1,0:T(8,128)}), f32[192,128]{1,0:T(8,128)}) %all-reduce.5.cloned.1.call-update) | async-done | bytes 98320 | tf_op jit(solution)/shard_map/psum | solution.py:48
  223.5 1.5 fusion
  225.0 1.0 copy-done.5
  226.0 1.1 fusion.18
  227.5 0.6 fusion.54
  228.8 39.1 %all-reduce.9.cloned.1.call-done = (f32[192,128]{1,0:T(8,128)}, f32[192,128]{1,0:T(8,128)}) async-done(((f32[192,128]{1,0:T(8,128)}, f32[192,128]{1,0:T(8,128)}), (f32[192,128]{1,0:T(8,128)}, f32[192,128]{1,0:T(8,128)})) %all-reduce.9.cloned.1.call-update) | async-done | bytes 196624 | tf_op jit(solution)/shard_map/psum | solution.py:52
  267.9 1.0 fusion.27
  268.9 1.5 convolution_convert_fusion
  270.4 1.7 copy.74
  272.2 0.5 fusion.2
  273.1 0.6 convolution_convert_fusion.1
  274.1 1.7 copy.73
  275.9 4.5 pad_maximum_fusion.1
  280.3 13.6 %all-to-all-start.3 = ((bf16[2,32,96,128]{3,0,2,1:T(2,128)(2,1)}), bf16[2,32,96,128]{3,0,2,1:T(2,128)(2,1)S(1)}, u32[]{:S(2)}, u32[]{:S(2)}) async-start(bf16[2,32,96,128]{3,0,2,1:T(2,128)(2,1)} %pad_maximum_fusion.1), calls=%async_computation.4 | async-start | bytes 3145728 | tf_op jit(solution)/shard_map/all_to_all | solution.py:115
  294.2 2.4 fusion.17
  296.6 2.9 convolution_convert_fusion.2
  299.4 37.7 %all-reduce.7.cloned.1.call-done = f32[192,128]{1,0:T(8,128)} async-done(((f32[192,128]{1,0:T(8,128)}), f32[192,128]{1,0:T(8,128)}) %all-reduce.7.cloned.1.call-update) | async-done | bytes 98320 | tf_op jit(solution)/shard_map/psum | solution.py:52
  337.2 2.2 fusion.3
  339.4 1.6 copy.70
  341.2 2.8 copy.71
  344.0 26.0 %all-to-all-done.3 = bf16[2,32,96,128]{3,0,2,1:T(2,128)(2,1)S(1)} async-done(((bf16[2,32,96,128]{3,0,2,1:T(2,128)(2,1)}), bf16[2,32,96,128]{3,0,2,1:T(2,128)(2,1)S(1)}, u32[]{:S(2)}, u32[]{:S(2)}) %all-to-all-start.3) | async-done | bytes 1572896 | tf_op jit(solution)/shard_map/all_to_all | solution.py:115
  369.9 5.8 %all-to-all-start.2 = ((bf16[2,32,96,128]{3,0,2,1:T(2,128)(2,1)}), bf16[2,32,96,128]{3,0,2,1:T(2,128)(2,1)S(1)}, u32[]{:S(2)}, u32[]{:S(2)}) async-start(bf16[2,32,96,128]{3,0,2,1:T(2,128)(2,1)} %copy.71), calls=%async_computation.2 | async-start | bytes 3145728 | tf_op jit(solution)/shard_map/all_to_all | solution.py:114
  375.8 1.8 fusion.13
  377.7 73.2 %all-to-all-done.2 = bf16[2,32,96,128]{3,0,2,1:T(2,128)(2,1)S(1)} async-done(((bf16[2,32,96,128]{3,0,2,1:T(2,128)(2,1)}), bf16[2,32,96,128]{3,0,2,1:T(2,128)(2,1)S(1)}, u32[]{:S(2)}, u32[]{:S(2)}) %all-to-all-start.2) | async-done | bytes 1572896 | tf_op jit(solution)/shard_map/all_to_all | solution.py:114
  450.9 1.8 fusion.10
  453.4 14.6 %reduce-scatter.5.cloned.1.call-done = f32[12,12,128]{2,0,1:T(8,128)} async-done(((f32[12,96,128]{2,0,1:T(8,128)}), f32[12,12,128]{2,0,1:T(8,128)}) %reduce-scatter.5.cloned.1.call-update) | async-done | bytes 73744 | tf_op jit(solution)/shard_map/reduce_scatter | solution.py:129
  468.0 0.9 divide_bitcast_fusion
  468.9 0.7 copy.77
  469.7 89.2 %reduce-scatter.3.cloned.1.call-done = f32[12,12,128]{2,0,1:T(8,128)} async-done(((f32[12,96,128]{2,0,1:T(8,128)}), f32[12,12,128]{2,0,1:T(8,128)}) %reduce-scatter.3.cloned.1.call-update) | async-done | bytes 73744 | tf_op jit(solution)/shard_map/reduce_scatter | solution.py:128
  558.9 0.9 divide_bitcast_fusion.1
  559.8 0.7 copy.76
  (53 shorter events, 2.6 us)
Async XLA Ops:
  7.2 2.0 copy-start
  9.2 1.0 copy-start.1
  109.0 4.2 copy-start.15
  109.0 78.8 %all-to-all-start.1 = ((bf16[32,2,96,128]{3,2,1,0:T(8,128)(2,1)}), bf16[32,2,96,128]{3,2,1,0:T(8,128)(2,1)S(1)}, u32[]{:S(2)}, u32[]{:S(2)}) async-start(bf16[32,2,96,128]{3,2,1,0:T(8,128)(2,1)} %get-tuple-element.21), calls=%async_computation.1 | async-start | bytes 3145728 | tf_op jit(solution)/shard_map/all_to_all | solution.py:83
  113.1 110.3 %all-reduce.5.cloned.1.call-start = ((), (), s32[]{:S(2)}) async-start(), calls=%async_computation.6 | async-start | bytes 196608 | tf_op jit(solution)/shard_map/psum | solution.py:48
  187.9 1.8 copy-start.3
  188.0 1.2 copy-start.9
  188.0 2.9 copy-start.6
  190.8 77.0 %all-reduce.9.cloned.1.call-start = ((), (), s32[]{:S(2)}) async-start(), calls=%async_computation.10 | async-start | bytes 393216 | tf_op jit(solution)/shard_map/psum | solution.py:52
  223.5 2.5 copy-start.10
  225.0 1.0 copy-start.5
  226.0 1.3 copy-start.2
  268.9 3.3 copy-start.14
  270.4 1.8 copy-start.11
  272.2 0.9 copy-start.13
  273.1 1.0 copy-start.12
  280.3 13.9 %copy-start.7 = (bf16[1,2,32,96,128]{4,3,2,1,0:T(8,128)(2,1)S(1)}, bf16[1,2,32,96,128]{4,3,2,1,0:T(8,128)(2,1)}, u32[]{:S(2)}) copy-start(bf16[1,2,32,96,128]{4,3,2,1,0:T(8,128)(2,1)} %copy.66) | copy-start | bytes 4718596
  280.3 89.6 %all-to-all-start.3 = ((bf16[2,32,96,128]{3,0,2,1:T(2,128)(2,1)}), bf16[2,32,96,128]{3,0,2,1:T(2,128)(2,1)S(1)}, u32[]{:S(2)}, u32[]{:S(2)}) async-start(bf16[2,32,96,128]{3,0,2,1:T(2,128)(2,1)} %pad_maximum_fusion.1), calls=%async_computation.4 | async-start | bytes 3145728 | tf_op jit(solution)/shard_map/all_to_all | solution.py:115
  293.9 43.3 %all-reduce.7.cloned.1.call-start = ((), (), s32[]{:S(2)}) async-start(), calls=%async_computation.7 | async-start | bytes 196608 | tf_op jit(solution)/shard_map/psum | solution.py:52
  296.5 40.7 %copy-start.4 = (bf16[1,1,4,48,3072]{4,3,2,1,0:T(8,128)(2,1)S(1)}, bf16[1,1,4,48,3072]{4,3,2,1,0:T(8,128)(2,1)}, u32[]{:S(2)}) copy-start(bf16[1,1,4,48,3072]{4,3,2,1,0:T(8,128)(2,1)} %param.9) | copy-start | bytes 3538948
  339.4 1.6 copy-start.8
  369.9 81.0 %all-to-all-start.2 = ((bf16[2,32,96,128]{3,0,2,1:T(2,128)(2,1)}), bf16[2,32,96,128]{3,0,2,1:T(2,128)(2,1)S(1)}, u32[]{:S(2)}, u32[]{:S(2)}) async-start(bf16[2,32,96,128]{3,0,2,1:T(2,128)(2,1)} %copy.71), calls=%async_computation.2 | async-start | bytes 3145728 | tf_op jit(solution)/shard_map/all_to_all | solution.py:114
  375.7 92.3 %reduce-scatter.5.cloned.1.call-start = ((), (), s32[]{:S(2)}) async-start(), calls=%async_computation.9 | async-start | bytes 884736 | tf_op jit(solution)/shard_map/reduce_scatter | solution.py:129
  377.7 181.2 %reduce-scatter.3.cloned.1.call-start = ((), (), s32[]{:S(2)}) async-start(), calls=%async_computation.8 | async-start | bytes 884736 | tf_op jit(solution)/shard_map/reduce_scatter | solution.py:128
Sparse Core Ops, SparseCore 0:
  190.9 32.4 all-reduce.4
  227.3 40.5 all-reduce.8
  297.6 39.5 all-reduce.6
  380.7 87.2 reduce-scatter.4
  473.0 85.8 reduce-scatter.2
where the time goes:
time: 568 us; the launch traced here: 567 us
  waiting for transfers between devices  379 us (67%)
  blocking collectives  94.1 us (17%)
  starting transfers between devices  23.9 us (4%)
  matrix products  19.9 us (4%)
  local copies, waits for them, and re-layouts  18.2 us (3%)
  other arithmetic  16.5 us (3%)
  between operations  15.4 us (3%)
    all_to_all x1, blocking collectives, local(): lax.all_to_all(send_up, 'pipe', split_axis=0, concat_axis=2, tiled=True)  94.1 us
    reduce_scatter x1, waiting for transfers between devices, local(): lax.psum_scatter(table_down, 'section', scatter_dimension=1, tiled=True)  89.2 us
    psum x2, waiting for transfers between devices, hidden_back(): lax.psum(jnp.dot(incoming, weight, preferred_element_type=jnp.float32), '...  76.8 us
    all_to_all x1, waiting for transfers between devices, local(): lax.all_to_all(stacked_down, 'pipe', split_axis=1, concat_axis=0, tiled=T...  73.2 us
    all_to_all x1, waiting for transfers between devices, local(): lax.all_to_all(send_down, 'pipe', split_axis=0, concat_axis=2, tiled=True)  69 us
    psum x1, waiting for transfers between devices, hidden_pre(): lax.psum(jnp.dot(section_rows, weight, preferred_element_type=jnp.float32...  30.2 us
    all_to_all x1, waiting for transfers between devices, local(): lax.all_to_all(stacked_up, 'pipe', split_axis=1, concat_axis=0, tiled=True)  26 us
    reduce_scatter x1, waiting for transfers between devices, local(): lax.psum_scatter(table_up, 'section', scatter_dimension=1, tiled=True)  14.6 us
  transfers between devices with their start and end apart: 8, of which 8 were waited for; matrix products, arithmetic and copies ran while one was open for 5% of the time, Pallas kernels for 0%

commit v1 on v0

v1 whole, which is shorter than its diff:
```python
import jax
import jax.numpy as jnp
import numpy as np
from jax import lax
from jax.experimental import pallas as pl
from jax.experimental.pallas import tpu as pltpu
from jax.sharding import PartitionSpec as P

MESH = pl.DeviceIdType.MESH
F32 = jnp.float32
BF16 = jnp.bfloat16

LAYERS = 12
SECTIONS = 8
ZS = 16
SIDE = 4
PLANE = 16
ROWS = 192
HALF = 3072
UNIT = 16
CHUNK = 384
CHUNKS = HALF // CHUNK
SLAB = 48
VMEM_LIMIT = 50 * 2**20

OFFSETS = (
    (1, 0), (0, 1), (3, 0), (0, 3), (2, 0), (0, 2), (1, 1), (3, 3),
    (1, 3), (3, 1), (2, 1), (1, 2), (2, 3), (3, 2), (2, 2),
)

gelu_scale = 0.7978845608028654
gelu_cubic = 0.044715


def gelu_pair(values):
    inner = jnp.tanh(gelu_scale * (values + gelu_cubic * values * values * values))
    value = 0.5 * values * (1.0 + inner)
    slope = 0.5 * (1.0 + inner) + 0.5 * values * (1.0 - inner * inner) * gelu_scale * (
        1.0 + 3.0 * gelu_cubic * values * values
    )
    return value, slope


def place():
    pipe = lax.axis_index("pipe")
    section = lax.axis_index("section")
    z, x_lo = pipe // 2, pipe % 2
    x, y = (section // SIDE) * 2 + x_lo, section % SIDE
    return z, x, y, x_lo, section


def chip(z, x, y):
    return {"pipe": z * 2 + x % 2, "section": (x // 2) * SIDE + y}


def seat(x, y):
    return (x % 2) * SECTIONS + (x // 2) * SIDE + y


def plane_steps(x, y):
    core = lax.axis_index("tensor")
    for a, b in OFFSETS:
        yield (x + a + core * (b - a)) % SIDE, (y + b + core * (a - b)) % SIDE


def greet(z, x, y):
    barrier = pltpu.get_barrier_semaphore()
    for tx, ty in plane_steps(x, y):
        pl.semaphore_signal(barrier, inc=1, device_id=chip(z, tx, ty), device_id_type=MESH)
    for step in (1, ZS - 1):
        pl.semaphore_signal(
            barrier, inc=1, device_id=chip((z + step) % ZS, x, y), device_id_type=MESH
        )


def greeted():
    pl.semaphore_wait(pltpu.get_barrier_semaphore(), PLANE - 1 + 2)


def remote(src, dst, send_sem, recv_sem, target):
    return pltpu.make_async_remote_copy(
        src_ref=src, dst_ref=dst, send_sem=send_sem, recv_sem=recv_sem,
        device_id=target, device_id_type=MESH,
    )


def wait_bytes(ref, sem):
    pltpu.make_async_copy(ref, ref, sem).wait()


def share(section, z):
    return (section + 2 * (z % 4)) % 8


def weights_kernel(
    tmpl_ref, split_ref, down_ref, up_ref, got_ref,
    layer_at, ring, work, stage, ring_send, ring_recv, send_sem, recv_sem,
):
    z, x, y, x_lo, section = place()
    greet(z, x, y)
    for lo in range(2):
        template = tmpl_ref[2 * z + lo]
        first = jnp.int32(0)
        for s in range(SECTIONS):
            layer_at[(lo * SECTIONS + s) * 2] = first
            layer_at[(lo * SECTIONS + s) * 2 + 1] = jnp.minimum(first + 1, LAYERS - 1)
            first = first + split_ref[template, s]
    own = pl.ds(pl.multiple_of(jnp.minimum(share(section, z), 5) * UNIT, UNIT), UNIT)
    for layer in range(LAYERS):
        for way in range(2):
            ring[way, 0, layer] = down_ref[layer, own, :]
            ring[way, 0, LAYERS + layer] = up_ref[layer, own, :]
    greeted()
    me = seat(x, y)

    def carried(at):
        return share(section, at % ZS) < 6

    def ring_copy(way, step, half=None):
        part = slice(None) if half is None else pl.ds(half * LAYERS, LAYERS)
        return remote(
            ring.at[way, step - 1, part], ring.at[way, step, part],
            ring_send.at[way, step], ring_recv.at[way, step],
            chip((z + (1 if way == 0 else ZS - 1)) % ZS, x, y),
        )

    def back(way, step):
        return z - step + ZS if way == 0 else z + step

    def ring_start(step, halves=False):
        for way in range(2):
            @pl.when(carried(back(way, step - 1)))
            def _():
                ring_copy(way, step, way if halves else None).start()

    def ring_wait(step, halves=False):
        for way in range(2):
            @pl.when(carried(back(way, step)))
            def _():
                ring_copy(way, step, way if halves else None).wait_recv()

    def ring_sent(step, halves=False):
        for way in range(2):
            @pl.when(carried(back(way, step - 1)))
            def _():
                ring_copy(way, step, way if halves else None).wait_send()

    def hand_out(way, step, entry, last=False):
        at = back(way, step) % ZS

        @pl.when(carried(at))
        def _():
            if last:
                work[:LAYERS] = ring[0, step, :LAYERS]
                work[LAYERS:] = ring[1, step, LAYERS:]
            else:
                work[...] = ring[way, step]
            for target in range(PLANE):
                for slot in range(2):
                    layer = layer_at[target * 2 + slot]
                    stage[entry, target, slot] = work[layer]
                    stage[entry, target, 2 + slot] = work[LAYERS + layer]
            unit = (2 * at + x_lo) * 6 + share(section, at)
            got_ref[unit] = stage[entry, me]
            for tx, ty in plane_steps(x, y):
                remote(
                    stage.at[entry, seat(tx, ty)], got_ref.at[unit],
                    send_sem.at[entry], recv_sem.at[entry], chip(z, tx, ty),
                ).start()

    ring_start(1)
    hand_out(0, 0, 0)

    def middle(step, _):
        ring_wait(step)
        ring_start(step + 1)
        hand_out(0, step, 2 * step - 1)
        hand_out(1, step, 2 * step)
        return 0

    lax.fori_loop(1, 7, middle, 0)
    ring_wait(7)
    ring_start(8, True)
    hand_out(0, 7, 13)
    hand_out(1, 7, 14)
    ring_wait(8, True)
    hand_out(0, 8, 15, True)

    def finish(entry, _):
        step = (entry + 1) // 2
        at = jnp.where(entry % 2 == 1, z - step + ZS, z + step)

        @pl.when(carried(at))
        def _():
            wait_bytes(stage.at[entry, pl.ds(0, PLANE - 1)], send_sem.at[entry])
            wait_bytes(got_ref.at[pl.ds(0, 11)], recv_sem.at[entry])

        @pl.when(jnp.logical_not(carried(at)))
        def _():
            wait_bytes(got_ref.at[pl.ds(0, 12)], recv_sem.at[entry])

        return 0

    lax.fori_loop(0, ZS, finish, 0)

    def ring_finish(step, _):
        ring_sent(step)
        return 0

    lax.fori_loop(1, 8, ring_finish, 0)
    ring_sent(8, True)


def terms_kernel(
    tmpl_ref, split_ref, mb_ref, x_ref, cot_ref, got_ref, order_ref, out_ref,
    inc, input_one, cot_zero, turned, part, other, send_sem, recv_sem,
):
    pipe, section, core = lax.axis_index("pipe"), lax.axis_index("section"), lax.axis_index("tensor")
    barrier = pltpu.get_barrier_semaphore()
    pl.semaphore_signal(barrier, inc=1, device_id={"tensor": 1 - core}, device_id_type=MESH)
    live = mb_ref[pipe]
    holds_two = jnp.where(split_ref[tmpl_ref[pipe], section] > 1, 1.0, 0.0)

    def weight(kind, q):
        return got_ref[pl.ds(q * (CHUNK // UNIT), CHUNK // UNIT), kind].reshape(CHUNK, 128)

    def columns(q):
        return pl.ds(pl.multiple_of(q * CHUNK, CHUNK), CHUNK)

    def dot(a, b):
        return jnp.dot(a, b, preferred_element_type=F32)

    def dot_turned(a, b):
        return lax.dot_general(a, b, (((1,), (1,)), ((), ())), preferred_element_type=F32)

    def exchange(at, count):
        copy = remote(
            part.at[pl.ds(at, count)], other.at[pl.ds(at, count)],
            send_sem.at[at], recv_sem.at[at], {"tensor": 1 - core},
        )
        copy.start()
        copy.wait()
        return [part[at + i] + other[at + i] for i in range(count)]

    part[...] = jnp.zeros_like(part)

    def first(q, _):
        cols = columns(q)
        for m in range(4):
            keep = jnp.where(m < live, 1.0, 0.0)
            rows = pl.ds(m * SLAB, SLAB)
            inc[rows, cols] = (cot_ref[rows, cols].astype(F32) * keep).astype(BF16)
        part[0] += dot(x_ref[:, cols], weight(0, q))
        part[1] += dot(inc[:, cols], weight(3, q))
        return 0

    lax.fori_loop(0, CHUNKS, first, 0)
    pl.semaphore_wait(barrier, 1)
    pre_zero, back_one = exchange(0, 2)
    value, slope_at_zero = gelu_pair(pre_zero)
    act_zero = value.astype(BF16)
    act_zero_t = value.T.astype(BF16)

    def second(q, _):
        cols = columns(q)
        moved = x_ref[:, cols].astype(F32) + dot_turned(act_zero, weight(2, q))
        rounded = moved.astype(BF16)
        input_one[:, cols] = rounded
        part[2] += dot(rounded, weight(1, q))
        return 0

    lax.fori_loop(0, CHUNKS, second, 0)
    (pre_one,) = exchange(2, 1)
    value, slope = gelu_pair(pre_one)
    act_one_t = value.T.astype(BF16)
    slope_one_wide = back_one * slope * holds_two
    slope_one = slope_one_wide.astype(BF16)
    slope_one_t = slope_one_wide.T.astype(BF16)

    def third(q, _):
        cols = columns(q)
        moved = inc[:, cols].astype(F32) + dot_turned(slope_one, weight(1, q))
        rounded = moved.astype(BF16)
        cot_zero[:, cols] = rounded
        part[3] += dot(rounded, weight(2, q))
        turned[q, 128:, :CHUNK] = dot(slope_one_t, input_one[:, cols]).astype(BF16)
        turned[q, 128:, CHUNK:] = dot(act_one_t, inc[:, cols]).astype(BF16)
        return 0

    lax.fori_loop(0, CHUNKS, third, 0)
    (back_zero,) = exchange(3, 1)
    slope_zero_t = (back_zero * slope_at_zero).T.astype(BF16)

    def fourth(q, _):
        cols = columns(q)
        turned[q, :128, :CHUNK] = dot(slope_zero_t, x_ref[:, cols]).astype(BF16)
        turned[q, :128, CHUNK:] = dot(act_zero_t, cot_zero[:, cols]).astype(BF16)
        sorted_rows = dot_turned(order_ref[...], turned[q]).astype(BF16)
        for slot in range(2):
            out_ref[q, :, slot] = sorted_rows[:, slot * 128:(slot + 1) * 128].reshape(PLANE, SLAB, 128)
        return 0

    lax.fori_loop(0, CHUNKS, fourth, 0)


GROUPS = ((4,), (3, 5), (2, 6), (1, 7), (0,))
RUNS = ((1,), (2, 3), (4, 5), (6, 7), (8,))
BLOCK = LAYERS * 24


def sums_kernel(
    tmpl_ref, split_ref, mb_ref, terms_ref, down_ref, up_ref,
    source, landed, work, table, going, coming, total,
    send_sem, recv_sem, ring_send, ring_recv,
):
    z, x, y, x_lo, section = place()
    greet(z, x, y)
    me = seat(x, y)
    for lo in range(2):
        template = tmpl_ref[2 * z + lo]
        firsts = []
        first = jnp.int32(0)
        for s in range(SECTIONS):
            firsts.append(first)
            first = first + split_ref[template, s]
        for layer in range(LAYERS):
            at, begins = jnp.int32(0), jnp.int32(0)
            for s in range(1, SECTIONS):
                at = jnp.where(firsts[s] <= layer, s, at)
                begins = jnp.where(firsts[s] <= layer, firsts[s], begins)
            slot = jnp.minimum(layer - begins, 1)
            source[lo * LAYERS + layer] = (lo * SECTIONS + at) * 2 + slot
    count = jnp.int32(0)
    for relay in range(2 * ZS):
        count = count + mb_ref[relay]
    greeted()

    def chunk_of(shift):
        return (z // 2 + shift) % CHUNKS

    def send_group(group):
        for tx, ty in plane_steps(x, y):
            for shift in group:
                q = chunk_of(shift)
                remote(
                    terms_ref.at[q, seat(tx, ty)], landed.at[q, me],
                    send_sem.at[shift], recv_sem.at[shift], chip(z, tx, ty),
                ).start()

    def add_up(shift):
        q = chunk_of(shift)
        landed[q, me] = terms_ref[q, me]
        wait_bytes(landed.at[q, pl.ds(0, PLANE - 1)], recv_sem.at[shift])
        work[...] = landed[q].reshape(2 * PLANE, SLAB, 128)
        for layer in range(LAYERS):
            both = work[source[layer]].astype(F32) + work[source[LAYERS + layer]].astype(F32)
            rows = pl.ds(layer * 24, 24)
            table[2 * q, rows] = both[:24]
            table[2 * q + 1, rows] = both[24:]

    HALF_BLOCK = BLOCK // 2

    def ring_copy(way, step):
        part = pl.ds(way * HALF_BLOCK, HALF_BLOCK) if step == 1 else slice(None)
        return remote(
            going.at[way, step - 1, part], coming.at[way, step - 1, part],
            ring_send.at[way, step - 1], ring_recv.at[way, step - 1],
            chip((z + (1 if way == 0 else ZS - 1)) % ZS, x, y),
        )

    def ring_step(step):
        far = 9 - step
        for way in range(2):
            to = (z + (far if way == 0 else ZS - far)) % ZS
            mine = pl.ds(way * HALF_BLOCK, HALF_BLOCK)
            if step == 1:
                going[way, 0, mine] = table[to, mine].astype(BF16)
            else:
                ring_copy(way, step - 1).wait_recv()
                if step == 2:
                    rest = pl.ds((1 - way) * HALF_BLOCK, HALF_BLOCK)
                    going[way, 1, mine] = (
                        table[to, mine] + coming[way, 0, mine].astype(F32)
                    ).astype(BF16)
                    going[way, 1, rest] = table[to, rest].astype(BF16)
                else:
                    going[way, step - 1] = (
                        table[to] + coming[way, step - 2].astype(F32)
                    ).astype(BF16)
            ring_copy(way, step).start()

    send_group(GROUPS[0])
    send_group(GROUPS[1])
    for turn, group in enumerate(GROUPS):
        for shift in group:
            add_up(shift)
        if turn + 2 < len(GROUPS):
            send_group(GROUPS[turn + 2])
        for step in RUNS[turn]:
            ring_step(step)
    ring_copy(0, 8).wait_recv()
    ring_copy(1, 8).wait_recv()
    scale = count.astype(F32)
    total[...] = (table[z] + coming[0, 7].astype(F32) + coming[1, 7].astype(F32)) / scale
    for layer in range(LAYERS):
        down_ref[layer] = total[layer * 24:layer * 24 + 12]
        up_ref[layer] = total[layer * 24 + 12:layer * 24 + 24]
    for step in range(1, 9):
        for way in range(2):
            ring_copy(way, step).wait_send()
    for shift in range(CHUNKS):
        wait_bytes(terms_ref.at[chunk_of(shift), pl.ds(0, PLANE - 1)], send_sem.at[shift])


def row_order():
    order = np.zeros((768, 768), np.float32)
    for lo in range(2):
        for s in range(SECTIONS):
            for near in range(2):
                for kind in range(2):
                    for j in range(12):
                        to = lo * 384 + s * 48 + near * 24 + kind * 12 + j
                        order[to, kind * 384 + (2 * near + lo) * 96 + s * 12 + j] = 1.0
    return order


def call(kernel, number, out_shape, spaces, scratch, *operands):
    many = isinstance(out_shape, (list, tuple))
    vmem = pl.BlockSpec(memory_space=pltpu.VMEM)
    return pl.pallas_call(
        kernel,
        out_shape=out_shape,
        in_specs=[pl.BlockSpec(memory_space=space) for space in spaces],
        out_specs=[vmem] * len(out_shape) if many else vmem,
        scratch_shapes=scratch,
        compiler_params=pltpu.CompilerParams(
            collective_id=number, has_side_effects=True, vmem_limit_bytes=VMEM_LIMIT
        ),
    )(*operands)


def local(stashed, cotangent, down_weight, up_weight, layer_split, template_of, mb_count):
    smem, vmem = pltpu.SMEM, pltpu.VMEM
    dma = pltpu.SemaphoreType.DMA
    got = call(
        weights_kernel, 1,
        jax.ShapeDtypeStruct((HALF // UNIT, 4, UNIT, 128), BF16),
        (smem, smem, vmem, vmem),
        [
            pltpu.SMEM((2 * PLANE,), jnp.int32),
            pltpu.VMEM((2, 9, 2 * LAYERS, UNIT, 128), BF16),
            pltpu.VMEM((2 * LAYERS, UNIT, 128), BF16),
            pltpu.VMEM((ZS, PLANE, 4, UNIT, 128), BF16),
            dma((2, 9)), dma((2, 9)), dma((ZS,)), dma((ZS,)),
        ],
        template_of, layer_split, down_weight[:, 0], up_weight[:, 0],
    )
    order = jnp.asarray(row_order(), BF16)
    terms = call(
        terms_kernel, 2,
        jax.ShapeDtypeStruct((CHUNKS, PLANE, 2, SLAB, 128), BF16),
        (smem, smem, smem, vmem, vmem, vmem, vmem),
        [
            pltpu.VMEM((ROWS, HALF), BF16),
            pltpu.VMEM((ROWS, HALF), BF16),
            pltpu.VMEM((ROWS, HALF), BF16),
            pltpu.VMEM((CHUNKS, 256, 2 * CHUNK), BF16),
            pltpu.VMEM((4, ROWS, 128), F32),
            pltpu.VMEM((4, ROWS, 128), F32),
            dma((4,)), dma((4,)),
        ],
        template_of, layer_split, mb_count,
        stashed.reshape(ROWS, HALF), cotangent.reshape(ROWS, HALF), got, order,
    )
    grad = jax.ShapeDtypeStruct((LAYERS, 12, 128), F32)
    grad_down, grad_up = call(
        sums_kernel, 3,
        [grad, grad],
        (smem, smem, smem, vmem),
        [
            pltpu.SMEM((2 * LAYERS,), jnp.int32),
            pltpu.VMEM((CHUNKS, PLANE, 2, SLAB, 128), BF16),
            pltpu.VMEM((2 * PLANE, SLAB, 128), BF16),
            pltpu.VMEM((ZS, BLOCK, 128), F32),
            pltpu.VMEM((2, 8, BLOCK, 128), BF16),
            pltpu.VMEM((2, 8, BLOCK, 128), BF16),
            pltpu.VMEM((BLOCK, 128), F32),
            dma((CHUNKS,)), dma((CHUNKS,)), dma((2, 8)), dma((2, 8)),
        ],
        template_of, layer_split, mb_count, terms,
    )
    return grad_down[:, None], grad_up[:, None]


def solution(mesh):
    placed = (
        P("pipe", "section", None, None, "tensor"),
        P("pipe", "section", None, None, "tensor"),
        P(None, "tensor", "pipe", None),
        P(None, "tensor", "pipe", None),
        P(),
        P(),
        P(),
    )
    return jax.shard_map(
        local,
        mesh=mesh,
        in_specs=placed,
        out_specs=(
            P(None, "tensor", ("pipe", "section"), None),
            P(None, "tensor", ("pipe", "section"), None),
        ),
        check_vma=False,
    )
```

time: 568 us -> 137 us (0.24)
  the two profiles are of different devices: /device:TPU:8 before, /device:TPU:4 now
where the time goes in v1:
time: 137 us; the launch traced here: 136 us
  Pallas kernels  127 us (93%)
  local copies, waits for them, and re-layouts  8.28 us (6%)
    pallas_call x3, Pallas kernels, call(): pl.pallas_call(kernel, out_shape=out_shape, in_specs=[pl.BlockSpec(memory...  127 us
    unnamed x21, local copies, waits for them, and re-layouts  8.28 us

profile of v1, /device:TPU:4, one launch (start us, length us, event | category | flops | bytes accessed | tf_op | source)
XLA Modules:
  0.0 136.3 jit_solution(8575141278585382802)
XLA Ops:
  0.6 0.8 copy.12.split_ref
  1.4 0.0 copy-start.5
  1.4 1.0 copy-done.5
  2.4 0.0 copy-start.6
  2.4 1.0 copy-done.6
  3.3 0.0 copy-start.7
  3.3 0.7 copy-done.7
  4.0 0.0 copy-start.2
  4.0 0.0 copy-start.3
  4.0 0.0 copy-start.4
  4.0 0.0 copy-start.8
  4.0 54.4 %shard_map.95.got_ref = bf16[192,4,16,128]{3,2,1,0:T(8,128)(2,1)S(1)} custom-call(s32[32]{0:T(128)S(1)} %copy-done.7, s32[16,8]{1,0:T(8,128)S(1)} %copy.12.split_ref, bf16[12,96,128]{2,1,0:T(8,128)(2,1)S(1)} %bitcast.8, bf16[12,96,128]{2,1,0:T(8,128)(2,1)S(1)} %bitcast.9), custom_call_target="tpu_custom_call" | custom-call | tf_op jit(solution)/shard_map/pallas_call | solution.py:430
  58.4 0.0 copy-start.1
  58.4 1.6 %copy-done.1 = bf16[192,4,16,128]{3,2,1,0:T(8,128)(2,1)} copy-done((bf16[192,4,16,128]{3,2,1,0:T(8,128)(2,1)}, bf16[192,4,16,128]{3,2,1,0:T(8,128)(2,1)S(1)}, u32[]{:S(2)}) %copy-start.1) | copy-done | bytes 3145752
  60.0 0.0 copy-done.2
  60.0 0.0 copy-done.3
  60.0 0.0 copy-done.4
  60.0 0.0 copy-done.8
  60.0 21.7 %shard_map.96.terms_ref = bf16[8,16,2,48,128]{4,3,2,1,0:T(8,128)(2,1)} custom-call(s32[32]{0:T(128)S(1)} %copy-done.7, s32[16,8]{1,0:T(8,128)S(1)} %copy.12.split_ref, s32[32]{0:T(128)S(1)} %copy-done.8, bf16[192,3072]{1,0:T(8,128)(2,1)S(1)} %bitcast.6, bf16[192,3072]{1,0:T(8,128)(2,1)S(1)} %bitcast.7, bf16[192,4,16,128]{3,2,1,0:T(8,128)(2,1)} %copy-done.1, ...), custom_call_target="tpu_custom_call" | custom-call | tf_op jit(solution)/shard_map/pallas_call | solution.py:430
  81.7 0.0 copy-start
  81.7 1.9 %copy-done = bf16[8,16,2,48,128]{4,3,2,1,0:T(8,128)(2,1)S(1)} copy-done((bf16[8,16,2,48,128]{4,3,2,1,0:T(8,128)(2,1)S(1)}, bf16[8,16,2,48,128]{4,3,2,1,0:T(8,128)(2,1)}, u32[]{:S(2)}) %copy-start) | copy-done | bytes 3145752
  83.6 51.3 %shard_map.97 = (f32[12,12,128]{2,1,0:T(8,128)S(1)}, f32[12,12,128]{2,1,0:T(8,128)S(1)}) custom-call(s32[32]{0:T(128)S(1)} %copy-done.7, s32[16,8]{1,0:T(8,128)S(1)} %copy.12.split_ref, s32[32]{0:T(128)S(1)} %copy-done.8, bf16[8,16,2,48,128]{4,3,2,1,0:T(8,128)(2,1)S(1)} %copy-done), custom_call_target="tpu_custom_call" | custom-call | tf_op jit(solution)/shard_map/pallas_call | solution.py:430
  134.8 0.7 copy.13
  135.6 0.7 copy.14
Async XLA Ops:
  1.4 1.0 copy-start.5
  2.4 1.0 copy-start.6
  3.3 0.7 copy-start.7
  4.0 56.0 %copy-start.2 = (bf16[1,1,4,48,3072]{4,3,2,1,0:T(8,128)(2,1)S(1)}, bf16[1,1,4,48,3072]{4,3,2,1,0:T(8,128)(2,1)}, u32[]{:S(2)}) copy-start(bf16[1,1,4,48,3072]{4,3,2,1,0:T(8,128)(2,1)} %param.8) | copy-start | bytes 3538948
  4.0 56.0 %copy-start.3 = (bf16[1,1,4,48,3072]{4,3,2,1,0:T(8,128)(2,1)S(1)}, bf16[1,1,4,48,3072]{4,3,2,1,0:T(8,128)(2,1)}, u32[]{:S(2)}) copy-start(bf16[1,1,4,48,3072]{4,3,2,1,0:T(8,128)(2,1)} %param.9) | copy-start | bytes 3538948
  4.0 56.0 %copy-start.4 = (bf16[768,768]{1,0:T(8,128)(2,1)S(1)}, bf16[768,768]{1,0:T(8,128)(2,1)}, u32[]{:S(2)}) copy-start(bf16[768,768]{1,0:T(8,128)(2,1)} %constant.2.clone.order_ref) | copy-start | bytes 3538948
  4.0 56.0 %copy-start.8 = (s32[32]{0:T(128)S(1)}, s32[32]{0:T(128)}, u32[]{:S(2)}) copy-start(s32[32]{0:T(128)} %mb_ref.3) | copy-start | bytes 388
  58.4 1.6 %copy-start.1 = (bf16[192,4,16,128]{3,2,1,0:T(8,128)(2,1)}, bf16[192,4,16,128]{3,2,1,0:T(8,128)(2,1)S(1)}, u32[]{:S(2)}) copy-start(bf16[192,4,16,128]{3,2,1,0:T(8,128)(2,1)S(1)} %shard_map.95.got_ref) | copy-start | bytes 9437188
  81.7 1.9 %copy-start = (bf16[8,16,2,48,128]{4,3,2,1,0:T(8,128)(2,1)S(1)}, bf16[8,16,2,48,128]{4,3,2,1,0:T(8,128)(2,1)}, u32[]{:S(2)}) copy-start(bf16[8,16,2,48,128]{4,3,2,1,0:T(8,128)(2,1)} %shard_map.96.terms_ref) | copy-start | bytes 9437188

commit v2 on v0

v2 whole, which is shorter than its diff:
```python
import jax
import jax.numpy as jnp
import numpy as np
from jax import lax
from jax.experimental import pallas as pl
from jax.experimental.pallas import tpu as pltpu
from jax.sharding import PartitionSpec as P

MESH = pl.DeviceIdType.MESH
F32 = jnp.float32
BF16 = jnp.bfloat16

LAYERS = 12
SECTIONS = 8
ZS = 16
SIDE = 4
PLANE = 16
ROWS = 192
HALF = 3072
UNIT = 16
CHUNK = 384
CHUNKS = HALF // CHUNK
SLAB = 48
VMEM_LIMIT = 56 * 2**20

OFFSETS = (
    (1, 0), (0, 1), (3, 0), (0, 3), (2, 0), (0, 2), (1, 1), (3, 3),
    (1, 3), (3, 1), (2, 1), (1, 2), (2, 3), (3, 2), (2, 2),
)

gelu_scale = 0.7978845608028654
gelu_cubic = 0.044715


def gelu_pair(values):
    inner = jnp.tanh(gelu_scale * (values + gelu_cubic * values * values * values))
    value = 0.5 * values * (1.0 + inner)
    slope = 0.5 * (1.0 + inner) + 0.5 * values * (1.0 - inner * inner) * gelu_scale * (
        1.0 + 3.0 * gelu_cubic * values * values
    )
    return value, slope


def place():
    pipe = lax.axis_index("pipe")
    section = lax.axis_index("section")
    z, x_lo = pipe // 2, pipe % 2
    x, y = (section // SIDE) * 2 + x_lo, section % SIDE
    return z, x, y, x_lo, section


def chip(z, x, y):
    return {"pipe": z * 2 + x % 2, "section": (x // 2) * SIDE + y}


def seat(x, y):
    return (x % 2) * SECTIONS + (x // 2) * SIDE + y


def plane_steps(x, y):
    core = lax.axis_index("tensor")
    for a, b in OFFSETS:
        yield (x + a + core * (b - a)) % SIDE, (y + b + core * (a - b)) % SIDE


def remote(src, dst, send_sem, recv_sem, target):
    return pltpu.make_async_remote_copy(
        src_ref=src, dst_ref=dst, send_sem=send_sem, recv_sem=recv_sem,
        device_id=target, device_id_type=MESH,
    )


def wait_bytes(ref, sem):
    pltpu.make_async_copy(ref, ref, sem).wait()


def share(section, z):
    return (section + 2 * (z % 4)) % 8


def dot(a, b):
    return jnp.dot(a, b, preferred_element_type=F32)


def dot_turned(a, b):
    return lax.dot_general(a, b, (((1,), (1,)), ((), ())), preferred_element_type=F32)


LAST = 15
BLOCK = LAYERS * 24
HALF_BLOCK = BLOCK // 2
HALF_LAYERS = LAYERS // 2


def kernel(
    tmpl_ref, split_ref, mb_ref, x_hbm, cot_hbm, down_hbm, up_hbm, order_hbm, grad_down_ref, grad_up_ref,
    layer_at, source, x_ref, cot_ref, order_ref, blocks, work, stage, got,
    inc, input_one, cot_zero, turned, part, other, terms, landed, gathered, table,
    far_go, near_go, far_in, near_in, total,
    local_sem, z_send, z_recv, hand_send, hand_recv, pair_send, pair_recv,
    term_send, term_recv, sum_send, sum_recv,
):
    z, x, y, x_lo, section = place()
    core = lax.axis_index("tensor")
    me = seat(x, y)
    odd = z % 2
    targets = [(seat(tx, ty), chip(z, tx, ty)) for tx, ty in plane_steps(x, y)]

    def column(step):
        return chip((z + step + 2 * ZS) % ZS, x, y)

    pair = {"tensor": 1 - core}
    barrier = pltpu.get_barrier_semaphore()
    for _, device in targets:
        pl.semaphore_signal(barrier, inc=1, device_id=device, device_id_type=MESH)
    for step in (1, -1, 2, -2):
        pl.semaphore_signal(barrier, inc=1, device_id=column(step), device_id_type=MESH)
    pl.semaphore_signal(barrier, inc=1, device_id=pair, device_id_type=MESH)

    own = pl.ds(pl.multiple_of(jnp.minimum(share(section, z), 5) * UNIT, UNIT), UNIT)
    loads = [
        pltpu.make_async_copy(down_hbm.at[:, own], blocks.at[0, :, 0], local_sem.at[0]),
        pltpu.make_async_copy(up_hbm.at[:, own], blocks.at[0, :, 1], local_sem.at[1]),
        pltpu.make_async_copy(x_hbm, x_ref, local_sem.at[2]),
        pltpu.make_async_copy(cot_hbm, cot_ref, local_sem.at[3]),
        pltpu.make_async_copy(order_hbm, order_ref, local_sem.at[4]),
    ]
    for load in loads:
        load.start()

    loads[0].wait()
    loads[1].wait()
    pl.semaphore_wait(barrier, PLANE - 1 + 4 + 1)

    def carried(at):
        return share(section, at % ZS) < 6

    def behind(way, distance):
        return (z + ZS - distance) % ZS if way == 0 else (z + distance) % ZS

    def entry_at(way, distance):
        if isinstance(distance, int) and distance in (0, 8):
            return 0 if distance == 0 else LAST
        return jnp.where(distance == 0, 0, 2 * distance - 1 + way)

    def z_copy(way, step, half):
        part = pl.ds(half * HALF_LAYERS, HALF_LAYERS)
        return remote(
            blocks.at[entry_at(way, step - 1), part], blocks.at[entry_at(way, step), part],
            z_send.at[step, way, half], z_recv.at[step, way, half], column(1 if way == 0 else -1),
        )

    def z_each(step, half, action, arriving):
        for way in range(2):
            if isinstance(step, int) and step == 8 and way != half:
                continue

            @pl.when(carried(behind(way, step if arriving else step - 1)))
            def _():
                action(z_copy(way, step, half))

    def z_start(step, half):
        z_each(step, half, lambda copy: copy.start(), False)

    def z_arrived(step, half):
        z_each(step, half, lambda copy: copy.wait_recv(), True)

    def z_sent(step):
        for half in range(2):
            z_each(step, half, lambda copy: copy.wait_send(), False)

    def place_of(entry):
        distance = (entry + 1) // 2
        return jnp.where(entry % 2 == 1, z + ZS - distance, z + distance) % ZS

    def hand_out(entry):
        at = place_of(entry)

        @pl.when(carried(at))
        def _():
            work[...] = blocks[entry]
            for four in range(0, PLANE, 4):
                slots = [(target, slot) for target in range(four, four + 4) for slot in range(2)]
                cut = [work[layer_at[target * 2 + slot]] for target, slot in slots]
                for (target, slot), rows in zip(slots, cut):
                    stage[entry, target, slot] = rows
            unit = (2 * at + x_lo) * 6 + share(section, at)
            got[unit] = stage[entry, me]
            for where, device in targets:
                remote(
                    stage.at[entry, where], got.at[unit], hand_send.at[entry], hand_recv.at[entry], device
                ).start()

    def handed(entry):
        at = place_of(entry)

        @pl.when(carried(at))
        def _():
            wait_bytes(got.at[pl.ds(0, 11)], hand_recv.at[entry])

        @pl.when(jnp.logical_not(carried(at)))
        def _():
            wait_bytes(got.at[pl.ds(0, 12)], hand_recv.at[entry])

    def over(first, last, body):
        def step(index, _):
            body(index)
            return 0

        lax.fori_loop(first, last, step, 0)

    def chunk_of(m, side):
        return (z // 2 + odd + jnp.where(side == 0, m - 1, CHUNKS - m)) % CHUNKS

    def weight(slot, kind, q):
        return got[pl.ds(q * (CHUNK // UNIT), CHUNK // UNIT), slot, kind].reshape(CHUNK, 128)

    def columns(q):
        return pl.ds(pl.multiple_of(q * CHUNK, CHUNK), CHUNK)

    def begin(q):
        cols = columns(q)
        for m in range(4):
            keep = jnp.where(m < live, 1.0, 0.0)
            rows = pl.ds(m * SLAB, SLAB)
            inc[rows, cols] = (cot_ref[rows, cols].astype(F32) * keep).astype(BF16)
        part[0] += dot(x_ref[:, cols], weight(0, 0, q))
        part[1] += dot(inc[:, cols], weight(1, 1, q))

    for half in range(2):
        z_start(1, half)
    for lo in range(2):
        template = tmpl_ref[2 * z + lo]
        firsts = []
        first = jnp.int32(0)
        for s in range(SECTIONS):
            firsts.append(first)
            layer_at[(lo * SECTIONS + s) * 2] = jnp.minimum(first, LAYERS - 1)
            layer_at[(lo * SECTIONS + s) * 2 + 1] = jnp.minimum(first + 1, LAYERS - 1)
            first = first + split_ref[s, template]
        for layer in range(LAYERS):
            at, begins = jnp.int32(0), jnp.int32(0)
            for s in range(1, SECTIONS):
                at = jnp.where(firsts[s] <= layer, s, at)
                begins = jnp.where(firsts[s] <= layer, firsts[s], begins)
            slot = jnp.minimum(layer - begins, 1)
            source[lo * LAYERS + layer] = slot * PLANE + lo * SECTIONS + at
    live = mb_ref[2 * z + x_lo]
    holds_two = jnp.where(split_ref[section, tmpl_ref[2 * z + x_lo]] > 1, 1.0, 0.0)
    count = jnp.int32(0)
    for relay in range(2 * ZS):
        count = count + mb_ref[relay]

    hand_out(jnp.int32(0))

    def ring_step(step):
        for half in range(2):
            z_arrived(step, half)
            z_start(step + 1, half)
        hand_out(2 * step - 1)
        hand_out(2 * step)

    over(1, 7, ring_step)
    for half in range(2):
        z_arrived(7, half)
        z_start(8, half)
    hand_out(jnp.int32(13))
    hand_out(jnp.int32(14))
    for half in range(2):
        z_arrived(8, half)
    hand_out(jnp.int32(15))

    part[...] = jnp.zeros_like(part)
    for load in loads[2:]:
        load.wait()
    for m in range(1, 5):
        over(0 if m == 1 else 4 * m - 3, min(4 * m + 1, ZS), handed)
        over(0, 2, lambda side: begin(chunk_of(m, side)))

    def exchange(at, number):
        copy = remote(
            part.at[pl.ds(at, number)], other.at[pl.ds(at, number)], pair_send.at[at], pair_recv.at[at], pair
        )
        copy.start()
        copy.wait()
        return [part[at + i] + other[at + i] for i in range(number)]

    pre_zero, back_one = exchange(0, 2)
    value, slope_at_zero = gelu_pair(pre_zero)
    act_zero = value.astype(BF16)
    act_zero_t = value.T.astype(BF16)

    def second(q):
        cols = columns(q)
        moved = x_ref[:, cols].astype(F32) + dot_turned(act_zero, weight(0, 1, q))
        rounded = moved.astype(BF16)
        input_one[:, cols] = rounded
        part[2] += dot(rounded, weight(1, 0, q))

    over(0, CHUNKS, second)
    (pre_one,) = exchange(2, 1)
    value, slope = gelu_pair(pre_one)
    act_one_t = value.T.astype(BF16)
    slope_one_wide = back_one * slope * holds_two
    slope_one = slope_one_wide.astype(BF16)
    slope_one_t = slope_one_wide.T.astype(BF16)

    def give(slot, q):
        sorted_rows = dot_turned(order_ref[...], turned[...]).astype(BF16)
        terms[slot, q] = sorted_rows.reshape(PLANE, SLAB, 128)
        for where, device in targets:
            remote(
                terms.at[slot, q, where], landed.at[slot, q, me],
                term_send.at[slot, q], term_recv.at[slot, q], device,
            ).start()

    def third(step):
        q = chunk_of(4 - step // 2, step % 2)
        cols = columns(q)
        turned[:, :CHUNK] = dot(slope_one_t, input_one[:, cols]).astype(BF16)
        turned[:, CHUNK:] = dot(act_one_t, inc[:, cols]).astype(BF16)
        give(1, q)
        moved = inc[:, cols].astype(F32) + dot_turned(slope_one, weight(1, 0, q))
        rounded = moved.astype(BF16)
        cot_zero[:, cols] = rounded
        part[3] += dot(rounded, weight(0, 1, q))

    over(0, CHUNKS, third)
    (back_zero,) = exchange(3, 1)
    slope_zero_t = (back_zero * slope_at_zero).T.astype(BF16)

    def fourth(q):
        cols = columns(q)
        turned[:, :CHUNK] = dot(slope_zero_t, x_ref[:, cols]).astype(BF16)
        turned[:, CHUNK:] = dot(act_zero_t, cot_zero[:, cols]).astype(BF16)
        give(0, q)

    def add_up(q):
        for slot in range(2):
            landed[slot, q, me] = terms[slot, q, me]
            wait_bytes(landed.at[slot, q, pl.ds(0, PLANE - 1)], term_recv.at[slot, q])
            gathered[slot * PLANE:(slot + 1) * PLANE] = landed[slot, q]
        for two in range(0, LAYERS, 2):
            both = [
                gathered[source[layer]].astype(F32) + gathered[source[LAYERS + layer]].astype(F32)
                for layer in (two, two + 1)
            ]
            for layer, rows in zip((two, two + 1), both):
                table[2 * q, pl.ds(layer * 24, 24)] = rows[:24]
                table[2 * q + 1, pl.ds(layer * 24, 24)] = rows[24:]

    def sum_copy(m, far, way):
        i = 4 - m
        step = (1 + far) * (1 if way == 0 else -1)
        if not far:
            return remote(
                near_go.at[way, i], near_in.at[way, i], sum_send.at[way, i, 0], sum_recv.at[way, i, 0], column(step)
            )
        rows = pl.ds(way * HALF_BLOCK, HALF_BLOCK) if m == 4 else slice(None)
        return remote(
            far_go.at[way, i, rows], far_in.at[way, i, rows], sum_send.at[way, i, 1], sum_recv.at[way, i, 1], column(step)
        )

    def pass_on(m):
        i = 4 - m
        for way in range(2):
            near_go[way, i] = table[behind(1 - way, 2 * m - 1)].astype(BF16)
            sum_copy(m, 0, way).start()
        for way in range(2):
            to = behind(1 - way, 2 * m)
            mine = pl.ds(way * HALF_BLOCK, HALF_BLOCK)
            rest = pl.ds((1 - way) * HALF_BLOCK, HALF_BLOCK)
            if m == 4:
                far_go[way, 0, mine] = table[to, mine].astype(BF16)
            else:
                sum_copy(m + 1, 0, way).wait_recv()
                sum_copy(m + 1, 1, way).wait_recv()
                if m == 3:
                    far_go[way, 1, mine] = (
                        table[to, mine] + near_in[way, 0, mine].astype(F32) + far_in[way, 0, mine].astype(F32)
                    ).astype(BF16)
                    far_go[way, 1, rest] = (table[to, rest] + near_in[way, 0, rest].astype(F32)).astype(BF16)
                else:
                    far_go[way, i] = (
                        table[to] + near_in[way, i - 1].astype(F32) + far_in[way, i - 1].astype(F32)
                    ).astype(BF16)
            sum_copy(m, 1, way).start()

    over(0, 2, lambda side: fourth(chunk_of(4, side)))
    for m in range(4, 0, -1):
        if m > 1:
            over(0, 2, lambda side: fourth(chunk_of(m - 1, side)))
        over(0, 2, lambda side: add_up(chunk_of(m, side)))
        pass_on(m)
    result = table[z]
    for way in range(2):
        sum_copy(1, 0, way).wait_recv()
        sum_copy(1, 1, way).wait_recv()
        result = result + near_in[way, 3].astype(F32) + far_in[way, 3].astype(F32)
    total[...] = result / count.astype(F32)
    for layer in range(LAYERS):
        grad_down_ref[layer * 12:layer * 12 + 12] = total[layer * 24:layer * 24 + 12]
        grad_up_ref[layer * 12:layer * 12 + 12] = total[layer * 24 + 12:layer * 24 + 24]

    over(1, 8, z_sent)
    z_sent(8)
    for m in range(1, 5):
        for way in range(2):
            sum_copy(m, 0, way).wait_send()
            sum_copy(m, 1, way).wait_send()

    def left(entry):
        @pl.when(carried(place_of(entry)))
        def _():
            wait_bytes(stage.at[entry, pl.ds(0, PLANE - 1)], hand_send.at[entry])

    over(0, LAST + 1, left)

    def given(step):
        wait_bytes(terms.at[step // CHUNKS, step % CHUNKS, pl.ds(0, PLANE - 1)], term_send.at[step // CHUNKS, step % CHUNKS])

    over(0, 2 * CHUNKS, given)


def row_order():
    order = np.zeros((768, 768), np.float32)
    for lo in range(2):
        for s in range(SECTIONS):
            for near in range(2):
                for kind in range(2):
                    for j in range(12):
                        to = lo * 384 + s * 48 + near * 24 + kind * 12 + j
                        order[to, kind * 384 + (2 * near + lo) * 96 + s * 12 + j] = 1.0
    return order


def local(stashed, cotangent, down_weight, up_weight, layer_split, template_of, mb_count):
    smem, hbm = pl.BlockSpec(memory_space=pltpu.SMEM), pl.BlockSpec(memory_space=pl.ANY)
    dma = pltpu.SemaphoreType.DMA
    grad = jax.ShapeDtypeStruct((LAYERS * 12, 128), F32)
    grad_down, grad_up = pl.pallas_call(
        kernel,
        out_shape=[grad, grad],
        in_specs=[smem] * 3 + [hbm] * 5,
        out_specs=[pl.BlockSpec(memory_space=pltpu.VMEM)] * 2,
        scratch_shapes=[
            pltpu.SMEM((2 * PLANE,), jnp.int32),
            pltpu.SMEM((2 * LAYERS,), jnp.int32),
            pltpu.VMEM((ROWS, HALF), BF16),
            pltpu.VMEM((ROWS, HALF), BF16),
            pltpu.VMEM((768, 768), BF16),
            pltpu.VMEM((ZS, LAYERS, 2, UNIT, 128), BF16),
            pltpu.VMEM((LAYERS, 2, UNIT, 128), BF16),
            pltpu.VMEM((ZS, PLANE, 2, 2, UNIT, 128), BF16),
            pltpu.VMEM((HALF // UNIT, 2, 2, UNIT, 128), BF16),
            pltpu.VMEM((ROWS, HALF), BF16),
            pltpu.VMEM((ROWS, HALF), BF16),
            pltpu.VMEM((ROWS, HALF), BF16),
            pltpu.VMEM((128, 2 * CHUNK), BF16),
            pltpu.VMEM((4, ROWS, 128), F32),
            pltpu.VMEM((4, ROWS, 128), F32),
            pltpu.VMEM((2, CHUNKS, PLANE, SLAB, 128), BF16),
            pltpu.VMEM((2, CHUNKS, PLANE, SLAB, 128), BF16),
            pltpu.VMEM((2 * PLANE, SLAB, 128), BF16),
            pltpu.VMEM((ZS, BLOCK, 128), F32),
            pltpu.VMEM((2, 4, BLOCK, 128), BF16),
            pltpu.VMEM((2, 4, BLOCK, 128), BF16),
            pltpu.VMEM((2, 4, BLOCK, 128), BF16),
            pltpu.VMEM((2, 4, BLOCK, 128), BF16),
            pltpu.VMEM((BLOCK, 128), F32),
            dma((5,)), dma((9, 2, 2)), dma((9, 2, 2)), dma((ZS,)), dma((ZS,)), dma((4,)), dma((4,)),
            dma((2, CHUNKS)), dma((2, CHUNKS)), dma((2, 4, 2)), dma((2, 4, 2)),
        ],
        compiler_params=pltpu.CompilerParams(
            collective_id=1, has_side_effects=True, vmem_limit_bytes=VMEM_LIMIT
        ),
    )(
        template_of, layer_split.T, mb_count, stashed.reshape(ROWS, HALF), cotangent.reshape(ROWS, HALF),
        down_weight[:, 0], up_weight[:, 0], jnp.asarray(row_order(), BF16),
    )
    return grad_down.reshape(LAYERS, 1, 12, 128), grad_up.reshape(LAYERS, 1, 12, 128)


def solution(mesh):
    placed = (
        P("pipe", "section", None, None, "tensor"),
        P("pipe", "section", None, None, "tensor"),
        P(None, "tensor", "pipe", None),
        P(None, "tensor", "pipe", None),
        P(),
        P(),
        P(),
    )
    return jax.shard_map(
        local,
        mesh=mesh,
        in_specs=placed,
        out_specs=(
            P(None, "tensor", ("pipe", "section"), None),
            P(None, "tensor", ("pipe", "section"), None),
        ),
        check_vma=False,
    )
```

time: 568 us -> 116 us (0.20)
  the two profiles are of different devices: /device:TPU:8 before, /device:TPU:32 now
where the time goes in v2:
time: 116 us; the launch traced here: 115 us
  Pallas kernels  112 us (97%)
  local copies, waits for them, and re-layouts  3.05 us (3%)
    pallas_call x1, Pallas kernels, local(): pl.pallas_call(kernel, out_shape=[grad, grad], in_specs=[smem] * 3 + [hbm...  112 us
    unnamed x2, local copies, waits for them, and re-layouts  3.05 us

profile of v2, /device:TPU:32, one launch (start us, length us, event | category | flops | bytes accessed | tf_op | source)
XLA Modules:
  0.0 115.3 jit_solution(14887088350522990785)
XLA Ops:
  0.6 111.6 %shard_map.95 = (f32[144,128]{1,0:T(8,128)}, f32[144,128]{1,0:T(8,128)}) custom-call(s32[32]{0:T(128)} %tmpl_ref.1, s32[8,16]{1,0:T(8,128)} %bitcast.13, s32[32]{0:T(128)} %mb_ref.1, bf16[192,3072]{1,0:T(8,128)(2,1)} %bitcast.7, bf16[192,3072]{1,0:T(8,128)(2,1)} %bitcast.8, bf16[12,96,128]{2,1,0:T(8,128)(2,1)} %bitcast.9, bf16[12,96,128]{2,1,0:T(8,128)(2,1)} %bitcast.10, ...), custom_call_target="tpu_custom_call" | custom-call | tf_op jit(solution)/shard_map/pallas_call | solution.py:441
  112.2 1.5 %copy.16 = f32[12,1,12,128]{3,1,2,0:T(1,128)} copy(f32[12,1,12,128]{3,1,2,0:T(1,128)} %bitcast.12) | data formatting | bytes 147456
  113.8 1.5 %copy.17 = f32[12,1,12,128]{3,1,2,0:T(1,128)} copy(f32[12,1,12,128]{3,1,2,0:T(1,128)} %bitcast.11) | data formatting | bytes 147456

commit v3 on v2

--- a/solution.py
+++ b/solution.py
@@ -95,7 +95,7 @@
 def kernel(
     tmpl_ref, split_ref, mb_ref, x_hbm, cot_hbm, down_hbm, up_hbm, order_hbm, grad_down_ref, grad_up_ref,
     layer_at, source, x_ref, cot_ref, order_ref, blocks, work, stage, got,
-    inc, input_one, cot_zero, turned, part, other, terms, landed, gathered, table,
+    inc, turned, part, other, terms, landed, gathered, table,
     far_go, near_go, far_in, near_in, total,
     local_sem, z_send, z_recv, hand_send, hand_recv, pair_send, pair_recv,
     term_send, term_recv, sum_send, sum_recv,
@@ -224,8 +224,14 @@
             keep = jnp.where(m < live, 1.0, 0.0)
             rows = pl.ds(m * SLAB, SLAB)
             inc[rows, cols] = (cot_ref[rows, cols].astype(F32) * keep).astype(BF16)
-        part[0] += dot(x_ref[:, cols], weight(0, 0, q))
-        part[1] += dot(inc[:, cols], weight(1, 1, q))
+        down_zero, down_one, up_zero, up_one = [weight(slot, kind, q) for kind in range(2) for slot in range(2)]
+        ahead = dot(x_ref[:, cols], jnp.concatenate([down_zero, down_one], axis=1))
+        back = dot(inc[:, cols], jnp.concatenate([up_one, up_zero], axis=1))
+        for at, rows in enumerate((ahead[:, :128], ahead[:, 128:], back[:, :128], back[:, 128:])):
+            part[pl.ds(at * ROWS, ROWS)] += rows
+        part[pl.ds(4 * ROWS, 128)] += lax.dot_general(
+            up_zero, down_one, (((0,), (0,)), ((), ())), preferred_element_type=F32
+        )
 
     for half in range(2):
         z_start(1, half)
@@ -244,7 +250,7 @@
                 at = jnp.where(firsts[s] <= layer, s, at)
                 begins = jnp.where(firsts[s] <= layer, firsts[s], begins)
             slot = jnp.minimum(layer - begins, 1)
-            source[lo * LAYERS + layer] = slot * PLANE + lo * SECTIONS + at
+            source[lo * LAYERS + layer] = (lo * SECTIONS + at) * 2 + slot
     live = mb_ref[2 * z + x_lo]
     holds_two = jnp.where(split_ref[section, tmpl_ref[2 * z + x_lo]] > 1, 1.0, 0.0)
     count = jnp.int32(0)
@@ -277,69 +283,48 @@
         over(0 if m == 1 else 4 * m - 3, min(4 * m + 1, ZS), handed)
         over(0, 2, lambda side: begin(chunk_of(m, side)))
 
-    def exchange(at, number):
-        copy = remote(
-            part.at[pl.ds(at, number)], other.at[pl.ds(at, number)], pair_send.at[at], pair_recv.at[at], pair
-        )
-        copy.start()
-        copy.wait()
-        return [part[at + i] + other[at + i] for i in range(number)]
-
-    pre_zero, back_one = exchange(0, 2)
-    value, slope_at_zero = gelu_pair(pre_zero)
+    swap = remote(part, other, pair_send.at[0], pair_recv.at[0], pair)
+    swap.start()
+    swap.wait()
+
+    def whole(at, rows=ROWS):
+        where = pl.ds(at * ROWS, rows)
+        return part[where] + other[where]
+
+    through = whole(4, 128)
+    through_high = through.astype(BF16)
+    through_low = (through - through_high.astype(F32)).astype(BF16)
+    value, slope_at_zero = gelu_pair(whole(0))
     act_zero = value.astype(BF16)
     act_zero_t = value.T.astype(BF16)
-
-    def second(q):
-        cols = columns(q)
-        moved = x_ref[:, cols].astype(F32) + dot_turned(act_zero, weight(0, 1, q))
-        rounded = moved.astype(BF16)
-        input_one[:, cols] = rounded
-        part[2] += dot(rounded, weight(1, 0, q))
-
-    over(0, CHUNKS, second)
-    (pre_one,) = exchange(2, 1)
-    value, slope = gelu_pair(pre_one)
+    pre_one = whole(1) + (dot(act_zero, through_high) + dot(act_zero, through_low))
+    value, slope_at_one = gelu_pair(pre_one)
     act_one_t = value.T.astype(BF16)
-    slope_one_wide = back_one * slope * holds_two
+    slope_one_wide = whole(2) * slope_at_one * holds_two
     slope_one = slope_one_wide.astype(BF16)
     slope_one_t = slope_one_wide.T.astype(BF16)
-
-    def give(slot, q):
+    back_zero = whole(3) + (dot_turned(slope_one, through_high) + dot_turned(slope_one, through_low))
+    slope_zero_t = (back_zero * slope_at_zero).T.astype(BF16)
+
+    def give(q):
+        cols = columns(q)
+        inputs, incoming = x_ref[:, cols], inc[:, cols]
+        input_one = (inputs.astype(F32) + dot_turned(act_zero, weight(0, 1, q))).astype(BF16)
+        cot_zero = (incoming.astype(F32) + dot_turned(slope_one, weight(1, 0, q))).astype(BF16)
+        turned[:128, :CHUNK] = dot(slope_zero_t, inputs).astype(BF16)
+        turned[128:, :CHUNK] = dot(slope_one_t, input_one).astype(BF16)
+        turned[:128, CHUNK:] = dot(act_zero_t, cot_zero).astype(BF16)
+        turned[128:, CHUNK:] = dot(act_one_t, incoming).astype(BF16)
         sorted_rows = dot_turned(order_ref[...], turned[...]).astype(BF16)
-        terms[slot, q] = sorted_rows.reshape(PLANE, SLAB, 128)
+        for slot in range(2):
+            terms[q, :, slot] = sorted_rows[:, slot * 128:(slot + 1) * 128].reshape(PLANE, SLAB, 128)
         for where, device in targets:
-            remote(
-                terms.at[slot, q, where], landed.at[slot, q, me],
-                term_send.at[slot, q], term_recv.at[slot, q], device,
-            ).start()
-
-    def third(step):
-        q = chunk_of(4 - step // 2, step % 2)
-        cols = columns(q)
-        turned[:, :CHUNK] = dot(slope_one_t, input_one[:, cols]).astype(BF16)
-        turned[:, CHUNK:] = dot(act_one_t, inc[:, cols]).astype(BF16)
-        give(1, q)
-        moved = inc[:, cols].astype(F32) + dot_turned(slope_one, weight(1, 0, q))
-        rounded = moved.astype(BF16)
-        cot_zero[:, cols] = rounded
-        part[3] += dot(rounded, weight(0, 1, q))
-
-    over(0, CHUNKS, third)
-    (back_zero,) = exchange(3, 1)
-    slope_zero_t = (back_zero * slope_at_zero).T.astype(BF16)
-
-    def fourth(q):
-        cols = columns(q)
-        turned[:, :CHUNK] = dot(slope_zero_t, x_ref[:, cols]).astype(BF16)
-        turned[:, CHUNK:] = dot(act_zero_t, cot_zero[:, cols]).astype(BF16)
-        give(0, q)
+            remote(terms.at[q, where], landed.at[q, me], term_send.at[q], term_recv.at[q], device).start()
 
     def add_up(q):
-        for slot in range(2):
-            landed[slot, q, me] = terms[slot, q, me]
-            wait_bytes(landed.at[slot, q, pl.ds(0, PLANE - 1)], term_recv.at[slot, q])
-            gathered[slot * PLANE:(slot + 1) * PLANE] = landed[slot, q]
+        landed[q, me] = terms[q, me]
+        wait_bytes(landed.at[q, pl.ds(0, PLANE - 1)], term_recv.at[q])
+        gathered[...] = landed[q].reshape(2 * PLANE, SLAB, 128)
         for two in range(0, LAYERS, 2):
             both = [
                 gathered[source[layer]].astype(F32) + gathered[source[LAYERS + layer]].astype(F32)
@@ -386,10 +371,10 @@
                     ).astype(BF16)
             sum_copy(m, 1, way).start()
 
-    over(0, 2, lambda side: fourth(chunk_of(4, side)))
+    over(0, 2, lambda side: give(chunk_of(4, side)))
     for m in range(4, 0, -1):
         if m > 1:
-            over(0, 2, lambda side: fourth(chunk_of(m - 1, side)))
+            over(0, 2, lambda side: give(chunk_of(m - 1, side)))
         over(0, 2, lambda side: add_up(chunk_of(m, side)))
         pass_on(m)
     result = table[z]
@@ -416,10 +401,10 @@
 
     over(0, LAST + 1, left)
 
-    def given(step):
-        wait_bytes(terms.at[step // CHUNKS, step % CHUNKS, pl.ds(0, PLANE - 1)], term_send.at[step // CHUNKS, step % CHUNKS])
-
-    over(0, 2 * CHUNKS, given)
+    def given(q):
+        wait_bytes(terms.at[q, pl.ds(0, PLANE - 1)], term_send.at[q])
+
+    over(0, CHUNKS, given)
 
 
 def row_order():
@@ -454,13 +439,11 @@
             pltpu.VMEM((ZS, PLANE, 2, 2, UNIT, 128), BF16),
             pltpu.VMEM((HALF // UNIT, 2, 2, UNIT, 128), BF16),
             pltpu.VMEM((ROWS, HALF), BF16),
-            pltpu.VMEM((ROWS, HALF), BF16),
-            pltpu.VMEM((ROWS, HALF), BF16),
-            pltpu.VMEM((128, 2 * CHUNK), BF16),
-            pltpu.VMEM((4, ROWS, 128), F32),
-            pltpu.VMEM((4, ROWS, 128), F32),
-            pltpu.VMEM((2, CHUNKS, PLANE, SLAB, 128), BF16),
-            pltpu.VMEM((2, CHUNKS, PLANE, SLAB, 128), BF16),
+            pltpu.VMEM((256, 2 * CHUNK), BF16),
+            pltpu.VMEM((4 * ROWS + 128, 128), F32),
+            pltpu.VMEM((4 * ROWS + 128, 128), F32),
+            pltpu.VMEM((CHUNKS, PLANE, 2, SLAB, 128), BF16),
+            pltpu.VMEM((CHUNKS, PLANE, 2, SLAB, 128), BF16),
             pltpu.VMEM((2 * PLANE, SLAB, 128), BF16),
             pltpu.VMEM((ZS, BLOCK, 128), F32),
             pltpu.VMEM((2, 4, BLOCK, 128), BF16),
@@ -468,8 +451,8 @@
             pltpu.VMEM((2, 4, BLOCK, 128), BF16),
             pltpu.VMEM((2, 4, BLOCK, 128), BF16),
             pltpu.VMEM((BLOCK, 128), F32),
-            dma((5,)), dma((9, 2, 2)), dma((9, 2, 2)), dma((ZS,)), dma((ZS,)), dma((4,)), dma((4,)),
-            dma((2, CHUNKS)), dma((2, CHUNKS)), dma((2, 4, 2)), dma((2, 4, 2)),
+            dma((5,)), dma((9, 2, 2)), dma((9, 2, 2)), dma((ZS,)), dma((ZS,)), dma((1,)), dma((1,)),
+            dma((CHUNKS,)), dma((CHUNKS,)), dma((2, 4, 2)), dma((2, 4, 2)),
         ],
         compiler_params=pltpu.CompilerParams(
             collective_id=1, has_side_effects=True, vmem_limit_bytes=VMEM_LIMIT

time: 116 us -> 110 us (0.948)
  Pallas kernels: 112 us -> 106 us
    pallas_call x1, Pallas kernels: 112 us -> 106 us  [local(): pl.pallas_call(kernel, out_shape=[grad, grad], in_specs=[smem] * 3 + [hbm...]
where the time goes in v3:
time: 110 us
  Pallas kernels  106 us (96%)
  local copies, waits for them, and re-layouts  3.05 us (3%)
    pallas_call x1, Pallas kernels, local(): pl.pallas_call(kernel, out_shape=[grad, grad], in_specs=[smem] * 3 + [hbm...  106 us
    unnamed x2, local copies, waits for them, and re-layouts  3.05 us

profile of v3, /device:TPU:32, one launch (start us, length us, event | category | flops | bytes accessed | tf_op | source)
XLA Modules:
  0.0 109.8 jit_solution(10551907086087281949)
XLA Ops:
  0.6 106.1 %shard_map.95 = (f32[144,128]{1,0:T(8,128)}, f32[144,128]{1,0:T(8,128)}) custom-call(s32[32]{0:T(128)} %tmpl_ref.1, s32[8,16]{1,0:T(8,128)} %bitcast.13, s32[32]{0:T(128)} %mb_ref.1, bf16[192,3072]{1,0:T(8,128)(2,1)} %bitcast.7, bf16[192,3072]{1,0:T(8,128)(2,1)} %bitcast.8, bf16[12,96,128]{2,1,0:T(8,128)(2,1)} %bitcast.9, bf16[12,96,128]{2,1,0:T(8,128)(2,1)} %bitcast.10, ...), custom_call_target="tpu_custom_call" | custom-call | tf_op jit(solution)/shard_map/pallas_call | solution.py:426
  106.7 1.5 %copy.16 = f32[12,1,12,128]{3,1,2,0:T(1,128)} copy(f32[12,1,12,128]{3,1,2,0:T(1,128)} %bitcast.12) | data formatting | bytes 147456
  108.3 1.5 %copy.17 = f32[12,1,12,128]{3,1,2,0:T(1,128)} copy(f32[12,1,12,128]{3,1,2,0:T(1,128)} %bitcast.11) | data formatting | bytes 147456

commit v4 on v3

--- a/solution.py
+++ b/solution.py
@@ -24,8 +24,8 @@
 VMEM_LIMIT = 56 * 2**20
 
 OFFSETS = (
-    (1, 0), (0, 1), (3, 0), (0, 3), (2, 0), (0, 2), (1, 1), (3, 3),
-    (1, 3), (3, 1), (2, 1), (1, 2), (2, 3), (3, 2), (2, 2),
+    (2, 2), (1, 0), (0, 1), (2, 1), (1, 2), (3, 0), (0, 3), (2, 3),
+    (3, 2), (2, 0), (0, 2), (1, 1), (3, 3), (1, 3), (3, 1),
 )
 
 gelu_scale = 0.7978845608028654
@@ -93,7 +93,7 @@
 
 
 def kernel(
-    tmpl_ref, split_ref, mb_ref, x_hbm, cot_hbm, down_hbm, up_hbm, order_hbm, grad_down_ref, grad_up_ref,
+    tmpl_ref, split_ref, mb_ref, x_hbm, cot_hbm, down_hbm, up_hbm, order_hbm, grads_ref,
     layer_at, source, x_ref, cot_ref, order_ref, blocks, work, stage, got,
     inc, turned, part, other, terms, landed, gathered, table,
     far_go, near_go, far_in, near_in, total,
@@ -336,21 +336,25 @@
 
     def sum_copy(m, far, way):
         i = 4 - m
-        step = (1 + far) * (1 if way == 0 else -1)
         if not far:
             return remote(
-                near_go.at[way, i], near_in.at[way, i], sum_send.at[way, i, 0], sum_recv.at[way, i, 0], column(step)
+                near_go.at[way, i], near_in.at[way, i], sum_send.at[way, i, 0], sum_recv.at[way, i, 0], column(1 - 2 * way)
             )
         rows = pl.ds(way * HALF_BLOCK, HALF_BLOCK) if m == 4 else slice(None)
         return remote(
-            far_go.at[way, i, rows], far_in.at[way, i, rows], sum_send.at[way, i, 1], sum_recv.at[way, i, 1], column(step)
+            far_go.at[way, i, rows], far_in.at[way, i, rows], sum_send.at[way, i, 1], sum_recv.at[way, i, 1],
+            column(2 - 4 * way),
         )
+
+    def pass_near(m, way):
+        near_go[way, 4 - m] = table[(z + (2 * m - 1) * (1 - 2 * way) + ZS) % ZS].astype(BF16)
+        sum_copy(m, 0, way).start()
 
     def pass_on(m):
         i = 4 - m
-        for way in range(2):
-            near_go[way, i] = table[behind(1 - way, 2 * m - 1)].astype(BF16)
-            sum_copy(m, 0, way).start()
+        if m > 1:
+            for way in range(2):
+                pass_near(m, way)
         for way in range(2):
             to = behind(1 - way, 2 * m)
             mine = pl.ds(way * HALF_BLOCK, HALF_BLOCK)
@@ -371,12 +375,19 @@
                     ).astype(BF16)
             sum_copy(m, 1, way).start()
 
+    def turn(m, i):
+        return (i + 1 + odd) % 2 if m == 1 else i
+
     over(0, 2, lambda side: give(chunk_of(4, side)))
-    for m in range(4, 0, -1):
-        if m > 1:
-            over(0, 2, lambda side: give(chunk_of(m - 1, side)))
+    for m in range(4, 1, -1):
+        over(0, 2, lambda i: give(chunk_of(m - 1, turn(m - 1, i))))
         over(0, 2, lambda side: add_up(chunk_of(m, side)))
         pass_on(m)
+    add_up(chunk_of(1, 1 - odd))
+    pass_near(1, 1 - odd)
+    pass_on(1)
+    add_up(chunk_of(1, odd))
+    pass_near(1, odd)
     result = table[z]
     for way in range(2):
         sum_copy(1, 0, way).wait_recv()
@@ -384,8 +395,8 @@
         result = result + near_in[way, 3].astype(F32) + far_in[way, 3].astype(F32)
     total[...] = result / count.astype(F32)
     for layer in range(LAYERS):
-        grad_down_ref[layer * 12:layer * 12 + 12] = total[layer * 24:layer * 24 + 12]
-        grad_up_ref[layer * 12:layer * 12 + 12] = total[layer * 24 + 12:layer * 24 + 24]
+        grads_ref[0, layer * 12:layer * 12 + 12] = total[layer * 24:layer * 24 + 12]
+        grads_ref[1, layer * 12:layer * 12 + 12] = total[layer * 24 + 12:layer * 24 + 24]
 
     over(1, 8, z_sent)
     z_sent(8)
@@ -422,12 +433,11 @@
 def local(stashed, cotangent, down_weight, up_weight, layer_split, template_of, mb_count):
     smem, hbm = pl.BlockSpec(memory_space=pltpu.SMEM), pl.BlockSpec(memory_space=pl.ANY)
     dma = pltpu.SemaphoreType.DMA
-    grad = jax.ShapeDtypeStruct((LAYERS * 12, 128), F32)
-    grad_down, grad_up = pl.pallas_call(
+    grads = pl.pallas_call(
         kernel,
-        out_shape=[grad, grad],
+        out_shape=jax.ShapeDtypeStruct((2, LAYERS * 12, 128), F32),
         in_specs=[smem] * 3 + [hbm] * 5,
-        out_specs=[pl.BlockSpec(memory_space=pltpu.VMEM)] * 2,
+        out_specs=pl.BlockSpec(memory_space=pltpu.VMEM),
         scratch_shapes=[
             pltpu.SMEM((2 * PLANE,), jnp.int32),
             pltpu.SMEM((2 * LAYERS,), jnp.int32),
@@ -461,7 +471,7 @@
         template_of, layer_split.T, mb_count, stashed.reshape(ROWS, HALF), cotangent.reshape(ROWS, HALF),
         down_weight[:, 0], up_weight[:, 0], jnp.asarray(row_order(), BF16),
     )
-    return grad_down.reshape(LAYERS, 1, 12, 128), grad_up.reshape(LAYERS, 1, 12, 128)
+    return grads[0].reshape(LAYERS, 1, 12, 128), grads[1].reshape(LAYERS, 1, 12, 128)
 
 
 def solution(mesh):

time: 110 us -> 105 us (0.955)
  the two profiles are of different devices: /device:TPU:32 before, /device:TPU:16 now
where the time goes in v4:
time: 105 us
  Pallas kernels  103 us (98%)
  local copies, waits for them, and re-layouts  1.58 us (2%)
    pallas_call x1, Pallas kernels, local(): pl.pallas_call(kernel, out_shape=jax.ShapeDtypeStruct((2, LAYERS * 12, 12...  103 us

profile of v4, /device:TPU:16, one launch (start us, length us, event | category | flops | bytes accessed | tf_op | source)
XLA Modules:
  0.0 105.0 jit_solution(3269122487851525402)
XLA Ops:
  0.6 102.8 %shard_map.95 = f32[2,144,128]{2,1,0:T(8,128)} custom-call(s32[32]{0:T(128)} %tmpl_ref.1, s32[8,16]{1,0:T(8,128)} %bitcast.13, s32[32]{0:T(128)} %mb_ref.1, bf16[192,3072]{1,0:T(8,128)(2,1)} %bitcast.7, bf16[192,3072]{1,0:T(8,128)(2,1)} %bitcast.8, bf16[12,96,128]{2,1,0:T(8,128)(2,1)} %bitcast.9, bf16[12,96,128]{2,1,0:T(8,128)(2,1)} %bitcast.10, ...), custom_call_target="tpu_custom_call" | custom-call | tf_op jit(solution)/shard_map/pallas_call | solution.py:436
  103.5 1.6 %fusion = (f32[1,144,128]{2,1,0:T(8,128)}, f32[1,144,128]{2,1,0:T(8,128)}) fusion(f32[2,144,128]{2,1,0:T(8,128)} %shard_map.95), kind=kLoop, calls=%fused_computation | loop fusion | bytes 294912 | tf_op jit(solution)/shard_map/slice | solution.py:474

commit v5 on v4

--- a/solution.py
+++ b/solution.py
@@ -87,6 +87,7 @@
 
 
 LAST = 15
+SPARE = 8
 BLOCK = LAYERS * 24
 HALF_BLOCK = BLOCK // 2
 HALF_LAYERS = LAYERS // 2
@@ -110,12 +111,6 @@
         return chip((z + step + 2 * ZS) % ZS, x, y)
 
     pair = {"tensor": 1 - core}
-    barrier = pltpu.get_barrier_semaphore()
-    for _, device in targets:
-        pl.semaphore_signal(barrier, inc=1, device_id=device, device_id_type=MESH)
-    for step in (1, -1, 2, -2):
-        pl.semaphore_signal(barrier, inc=1, device_id=column(step), device_id_type=MESH)
-    pl.semaphore_signal(barrier, inc=1, device_id=pair, device_id_type=MESH)
 
     own = pl.ds(pl.multiple_of(jnp.minimum(share(section, z), 5) * UNIT, UNIT), UNIT)
     loads = [
@@ -128,113 +123,13 @@
     for load in loads:
         load.start()
 
-    loads[0].wait()
-    loads[1].wait()
-    pl.semaphore_wait(barrier, PLANE - 1 + 4 + 1)
-
-    def carried(at):
-        return share(section, at % ZS) < 6
-
-    def behind(way, distance):
-        return (z + ZS - distance) % ZS if way == 0 else (z + distance) % ZS
-
-    def entry_at(way, distance):
-        if isinstance(distance, int) and distance in (0, 8):
-            return 0 if distance == 0 else LAST
-        return jnp.where(distance == 0, 0, 2 * distance - 1 + way)
-
-    def z_copy(way, step, half):
-        part = pl.ds(half * HALF_LAYERS, HALF_LAYERS)
-        return remote(
-            blocks.at[entry_at(way, step - 1), part], blocks.at[entry_at(way, step), part],
-            z_send.at[step, way, half], z_recv.at[step, way, half], column(1 if way == 0 else -1),
-        )
-
-    def z_each(step, half, action, arriving):
-        for way in range(2):
-            if isinstance(step, int) and step == 8 and way != half:
-                continue
-
-            @pl.when(carried(behind(way, step if arriving else step - 1)))
-            def _():
-                action(z_copy(way, step, half))
-
-    def z_start(step, half):
-        z_each(step, half, lambda copy: copy.start(), False)
-
-    def z_arrived(step, half):
-        z_each(step, half, lambda copy: copy.wait_recv(), True)
-
-    def z_sent(step):
-        for half in range(2):
-            z_each(step, half, lambda copy: copy.wait_send(), False)
-
-    def place_of(entry):
-        distance = (entry + 1) // 2
-        return jnp.where(entry % 2 == 1, z + ZS - distance, z + distance) % ZS
-
-    def hand_out(entry):
-        at = place_of(entry)
-
-        @pl.when(carried(at))
-        def _():
-            work[...] = blocks[entry]
-            for four in range(0, PLANE, 4):
-                slots = [(target, slot) for target in range(four, four + 4) for slot in range(2)]
-                cut = [work[layer_at[target * 2 + slot]] for target, slot in slots]
-                for (target, slot), rows in zip(slots, cut):
-                    stage[entry, target, slot] = rows
-            unit = (2 * at + x_lo) * 6 + share(section, at)
-            got[unit] = stage[entry, me]
-            for where, device in targets:
-                remote(
-                    stage.at[entry, where], got.at[unit], hand_send.at[entry], hand_recv.at[entry], device
-                ).start()
-
-    def handed(entry):
-        at = place_of(entry)
-
-        @pl.when(carried(at))
-        def _():
-            wait_bytes(got.at[pl.ds(0, 11)], hand_recv.at[entry])
-
-        @pl.when(jnp.logical_not(carried(at)))
-        def _():
-            wait_bytes(got.at[pl.ds(0, 12)], hand_recv.at[entry])
-
-    def over(first, last, body):
-        def step(index, _):
-            body(index)
-            return 0
-
-        lax.fori_loop(first, last, step, 0)
-
-    def chunk_of(m, side):
-        return (z // 2 + odd + jnp.where(side == 0, m - 1, CHUNKS - m)) % CHUNKS
-
-    def weight(slot, kind, q):
-        return got[pl.ds(q * (CHUNK // UNIT), CHUNK // UNIT), slot, kind].reshape(CHUNK, 128)
-
-    def columns(q):
-        return pl.ds(pl.multiple_of(q * CHUNK, CHUNK), CHUNK)
-
-    def begin(q):
-        cols = columns(q)
-        for m in range(4):
-            keep = jnp.where(m < live, 1.0, 0.0)
-            rows = pl.ds(m * SLAB, SLAB)
-            inc[rows, cols] = (cot_ref[rows, cols].astype(F32) * keep).astype(BF16)
-        down_zero, down_one, up_zero, up_one = [weight(slot, kind, q) for kind in range(2) for slot in range(2)]
-        ahead = dot(x_ref[:, cols], jnp.concatenate([down_zero, down_one], axis=1))
-        back = dot(inc[:, cols], jnp.concatenate([up_one, up_zero], axis=1))
-        for at, rows in enumerate((ahead[:, :128], ahead[:, 128:], back[:, :128], back[:, 128:])):
-            part[pl.ds(at * ROWS, ROWS)] += rows
-        part[pl.ds(4 * ROWS, 128)] += lax.dot_general(
-            up_zero, down_one, (((0,), (0,)), ((), ())), preferred_element_type=F32
-        )
-
-    for half in range(2):
-        z_start(1, half)
+    barrier = pltpu.get_barrier_semaphore()
+    for _, device in targets:
+        pl.semaphore_signal(barrier, inc=1, device_id=device, device_id_type=MESH)
+    for step in (1, -1, 2, -2):
+        pl.semaphore_signal(barrier, inc=1, device_id=column(step), device_id_type=MESH)
+    pl.semaphore_signal(barrier, inc=1, device_id=pair, device_id_type=MESH)
+
     for lo in range(2):
         template = tmpl_ref[2 * z + lo]
         firsts = []
@@ -257,6 +152,113 @@
     for relay in range(2 * ZS):
         count = count + mb_ref[relay]
 
+    loads[0].wait()
+    loads[1].wait()
+    pl.semaphore_wait(barrier, PLANE - 1 + 4 + 1)
+
+    def carried(at):
+        return share(section, at % ZS) < 6
+
+    def behind(way, distance):
+        return (z + ZS - distance) % ZS if way == 0 else (z + distance) % ZS
+
+    def entry_at(way, distance):
+        if isinstance(distance, int) and distance in (0, 8):
+            return 0 if distance == 0 else LAST
+        return jnp.where(distance == 0, 0, 2 * distance - 1 + way)
+
+    def z_copy(way, step, half):
+        part = pl.ds(half * HALF_LAYERS, HALF_LAYERS)
+        return remote(
+            blocks.at[entry_at(way, step - 1), part], blocks.at[entry_at(way, step), part],
+            z_send.at[step, way, half], z_recv.at[step, way, half], column(1 if way == 0 else -1),
+        )
+
+    def z_each(step, half, action, arriving):
+        for way in range(2):
+            if isinstance(step, int) and step == 8 and way != half:
+                continue
+
+            @pl.when(carried(behind(way, step if arriving else step - 1)))
+            def _():
+                action(z_copy(way, step, half))
+
+    def z_start(step, half):
+        z_each(step, half, lambda copy: copy.start(), False)
+
+    def z_arrived(step, half):
+        z_each(step, half, lambda copy: copy.wait_recv(), True)
+
+    def z_sent(step):
+        for half in range(2):
+            z_each(step, half, lambda copy: copy.wait_send(), False)
+
+    def place_of(entry):
+        distance = (entry + 1) // 2
+        return jnp.where(entry % 2 == 1, z + ZS - distance, z + distance) % ZS
+
+    def hand_out(entry):
+        at = place_of(entry)
+
+        @pl.when(carried(at))
+        def _():
+            work[...] = blocks[entry]
+            for four in range(0, PLANE, 4):
+                slots = [(target, slot) for target in range(four, four + 4) for slot in range(2)]
+                cut = [work[layer_at[target * 2 + slot]] for target, slot in slots]
+                for (target, slot), rows in zip(slots, cut):
+                    stage[entry, target, slot] = rows
+            unit = (2 * at + x_lo) * 6 + share(section, at)
+            got[unit] = stage[entry, me]
+            for where, device in targets:
+                remote(
+                    stage.at[entry, where], got.at[unit], hand_send.at[entry], hand_recv.at[entry], device
+                ).start()
+
+    def handed(entry):
+        at = place_of(entry)
+
+        @pl.when(carried(at))
+        def _():
+            wait_bytes(got.at[pl.ds(0, 11)], hand_recv.at[entry])
+
+        @pl.when(jnp.logical_not(carried(at)))
+        def _():
+            wait_bytes(got.at[pl.ds(0, 12)], hand_recv.at[entry])
+
+    def over(first, last, body):
+        def step(index, _):
+            body(index)
+            return 0
+
+        lax.fori_loop(first, last, step, 0)
+
+    def chunk_of(m, side):
+        return (z // 2 + odd + jnp.where(side == 0, m - 1, CHUNKS - m)) % CHUNKS
+
+    def weight(slot, kind, q):
+        return got[pl.ds(q * (CHUNK // UNIT), CHUNK // UNIT), slot, kind].reshape(CHUNK, 128)
+
+    def columns(q):
+        return pl.ds(pl.multiple_of(q * CHUNK, CHUNK), CHUNK)
+
+    def begin(q):
+        cols = columns(q)
+        for m in range(4):
+            keep = jnp.where(m < live, 1.0, 0.0)
+            rows = pl.ds(m * SLAB, SLAB)
+            inc[rows, cols] = (cot_ref[rows, cols].astype(F32) * keep).astype(BF16)
+        down_zero, down_one, up_zero, up_one = [weight(slot, kind, q) for kind in range(2) for slot in range(2)]
+        ahead = dot(x_ref[:, cols], jnp.concatenate([down_zero, down_one], axis=1))
+        back = dot(inc[:, cols], jnp.concatenate([up_one, up_zero], axis=1))
+        for at, rows in enumerate((ahead[:, :128], ahead[:, 128:], back[:, :128], back[:, 128:])):
+            part[pl.ds(at * ROWS, ROWS)] += rows
+        part[pl.ds(4 * ROWS, 128)] += lax.dot_general(
+            up_zero, down_one, (((0,), (0,)), ((), ())), preferred_element_type=F32
+        )
+
+    for half in range(2):
+        z_start(1, half)
     hand_out(jnp.int32(0))
 
     def ring_step(step):
@@ -280,8 +282,12 @@
     for load in loads[2:]:
         load.wait()
     for m in range(1, 5):
-        over(0 if m == 1 else 4 * m - 3, min(4 * m + 1, ZS), handed)
-        over(0, 2, lambda side: begin(chunk_of(m, side)))
+        over(0 if m == 1 else 4 * m - 3, 4 * m + 1 if m < 4 else LAST, handed)
+        if m < 4:
+            over(0, 2, lambda side: begin(chunk_of(m, side)))
+    begin(chunk_of(4, odd))
+    handed(jnp.int32(LAST))
+    begin(chunk_of(4, 1 - odd))
 
     swap = remote(part, other, pair_send.at[0], pair_recv.at[0], pair)
     swap.start()
@@ -393,7 +399,7 @@
         sum_copy(1, 0, way).wait_recv()
         sum_copy(1, 1, way).wait_recv()
         result = result + near_in[way, 3].astype(F32) + far_in[way, 3].astype(F32)
-    total[...] = result / count.astype(F32)
+    total[:BLOCK] = result / count.astype(F32)
     for layer in range(LAYERS):
         grads_ref[0, layer * 12:layer * 12 + 12] = total[layer * 24:layer * 24 + 12]
         grads_ref[1, layer * 12:layer * 12 + 12] = total[layer * 24 + 12:layer * 24 + 24]
@@ -435,7 +441,7 @@
     dma = pltpu.SemaphoreType.DMA
     grads = pl.pallas_call(
         kernel,
-        out_shape=jax.ShapeDtypeStruct((2, LAYERS * 12, 128), F32),
+        out_shape=jax.ShapeDtypeStruct((2, LAYERS * 12 + SPARE, 128), F32),
         in_specs=[smem] * 3 + [hbm] * 5,
         out_specs=pl.BlockSpec(memory_space=pltpu.VMEM),
         scratch_shapes=[
@@ -460,7 +466,7 @@
             pltpu.VMEM((2, 4, BLOCK, 128), BF16),
             pltpu.VMEM((2, 4, BLOCK, 128), BF16),
             pltpu.VMEM((2, 4, BLOCK, 128), BF16),
-            pltpu.VMEM((BLOCK, 128), F32),
+            pltpu.VMEM((BLOCK + SPARE, 128), F32),
             dma((5,)), dma((9, 2, 2)), dma((9, 2, 2)), dma((ZS,)), dma((ZS,)), dma((1,)), dma((1,)),
             dma((CHUNKS,)), dma((CHUNKS,)), dma((2, 4, 2)), dma((2, 4, 2)),
         ],
@@ -471,7 +477,8 @@
         template_of, layer_split.T, mb_count, stashed.reshape(ROWS, HALF), cotangent.reshape(ROWS, HALF),
         down_weight[:, 0], up_weight[:, 0], jnp.asarray(row_order(), BF16),
     )
-    return grads[0].reshape(LAYERS, 1, 12, 128), grads[1].reshape(LAYERS, 1, 12, 128)
+    grad_down, grad_up = grads[0, :LAYERS * 12], grads[1, :LAYERS * 12]
+    return grad_down.reshape(LAYERS, 1, 12, 128), grad_up.reshape(LAYERS, 1, 12, 128)
 
 
 def solution(mesh):

time: 105 us -> 105 us (level)
  the two profiles are of different devices: /device:TPU:16 before, /device:TPU:8 now
where the time goes in v5:
time: 105 us
  Pallas kernels  103 us (98%)
  local copies, waits for them, and re-layouts  1.58 us (2%)
    pallas_call x1, Pallas kernels, local(): pl.pallas_call(kernel, out_shape=jax.ShapeDtypeStruct((2, LAYERS * 12 + S...  103 us

profile of v5, /device:TPU:8, one launch (start us, length us, event | category | flops | bytes accessed | tf_op | source)
XLA Modules:
  0.0 105.0 jit_solution(8502427497211219924)
XLA Ops:
  0.6 102.8 %shard_map.95 = f32[2,152,128]{2,1,0:T(8,128)} custom-call(s32[32]{0:T(128)} %tmpl_ref.1, s32[8,16]{1,0:T(8,128)} %bitcast.13, s32[32]{0:T(128)} %mb_ref.1, bf16[192,3072]{1,0:T(8,128)(2,1)} %bitcast.7, bf16[192,3072]{1,0:T(8,128)(2,1)} %bitcast.8, bf16[12,96,128]{2,1,0:T(8,128)(2,1)} %bitcast.9, bf16[12,96,128]{2,1,0:T(8,128)(2,1)} %bitcast.10, ...), custom_call_target="tpu_custom_call" | custom-call | tf_op jit(solution)/shard_map/pallas_call | solution.py:442
  103.4 1.6 %fusion = (f32[1,144,128]{2,1,0:T(8,128)}, f32[1,144,128]{2,1,0:T(8,128)}) fusion(f32[2,152,128]{2,1,0:T(8,128)} %shard_map.95), kind=kLoop, calls=%fused_computation | loop fusion | bytes 294912 | tf_op jit(solution)/shard_map/slice | solution.py:480
